TPU v7x, 32 devices: a whole 2x2x4 slice. The times are simulated.
32 devices in a mesh: row: 8 (over y, x, core), col: 4 (over z).
Axes of the slice: x: 2, y: 2, z: 4, core: 2. Of those that a mesh axis runs over, the one named last changes fastest.
Arguments:
- hidden_states: bfloat16 [8192, 2048], P('row', 'col'), may hold values from -21 to 21
- lengths: int32 [16], P('row'), may hold values from 16 to 512, as said below
- qkvg_master: float32 [2048, 12288], P(('row', 'col')), may hold values from -0.125 to 0.125
- gateup_master: float32 [2, 2048, 4096], P(None, ('row', 'col')), may hold values from -0.125 to 0.125
- out_master: float32 [4096, 2048], P(None, ('row', 'col')), may hold values from -0.09375 to 0.09375
- down_master: float32 [4096, 2048], P(None, ('row', 'col')), may hold values from -0.09375 to 0.09375
Outputs:
- layer_output: bfloat16 [8192, 2048], P('row', 'col')
- qkvg_weight: bfloat16 [2048, 12288], P('row', 'col')
- gateup_weight: bfloat16 [2, 2048, 4096], P(None, 'row', 'col')
- mixing_weight: bfloat16 [4096, 2048], P('col', 'row')
- down_weight: bfloat16 [4096, 2048], P('col', 'row')
Inputs may be any that keep to these rules, and one draw needn't show every extreme that they name: `lengths`: prompt length of each request; the positions of a request from its length on are padding. Some request has length 512 in every draw.
All inputs are finite; a program needn't handle non-finite values.
Results may differ from a plain program's by a relative error of at most 0.014.
Values may be sent and summed in bfloat16 or wider, within the bound.
No kernel may reach another device: no remote copies, remote signals or barrier semaphores. Data moves between devices by JAX's collectives and lax.ppermute only.
A program may use at most 128 MiB of HBM per device.

v0:
```python
import functools
import math

import jax
import jax.numpy as jnp
from jax import lax
from jax.experimental import pallas as pl
from jax.experimental.pallas import tpu as pltpu
from jax.sharding import PartitionSpec as P

D = 2048
HEADS = 8
KEY = 256
VAL = 512
S = 512
TILE = 16
TILES = S // TILE
HEAD_WIDTH = 2 * KEY + 2 * VAL

epsilon = 1e-05
VMEM_LIMIT = 56 * 1024 * 1024

SMEM = pl.BlockSpec(memory_space=pltpu.SMEM)
VMEM = pl.BlockSpec(memory_space=pltpu.VMEM)
ANY = pl.BlockSpec(memory_space=pl.ANY)


def params():
    return pltpu.CompilerParams(vmem_limit_bytes=VMEM_LIMIT)


def cost(flops, moved):
    return pl.CostEstimate(flops=int(flops), bytes_accessed=int(moved), transcendentals=0)


def swap(block, axis, step):
    size = lax.axis_size(axis)
    return lax.ppermute(block, axis, [(i, i ^ step) for i in range(size)])


def after(value, *earlier):
    return lax.optimization_barrier((value,) + earlier)[0]


def gather_rows(block, direct=False, behind=()):
    size = lax.axis_size("row")
    pieces = {0: block}
    if size == 8:
        half = block.shape[0] // 2
        pieces[2] = swap(block, "row", 2)
        pieces[4] = swap(block, "row", 4)
        if direct:
            pieces[6] = swap(block, "row", 6)
        else:
            across, along = pieces[2], pieces[4]
            if behind:
                across, along = after((across, along), *behind)
            upper = swap(along[:half], "row", 2)
            lower = swap(across[half:], "row", 4)
            pieces[6] = jnp.concatenate([upper, lower], axis=0)
        bits = [1]
    else:
        bits = [1 << i for i in reversed(range(size.bit_length() - 1))]
    for bit in bits:
        for j in sorted(pieces):
            pieces[j | bit] = swap(pieces[j], "row", bit)
    return [pieces[j] for j in range(size)]


def last_parts(pieces):
    return (pieces[6], pieces[1], pieces[3], pieces[5]) if len(pieces) == 8 else (pieces[-1],)


def gather_lengths(lengths):
    size = lax.axis_size("row")
    bit = 1
    while bit < size:
        lengths = jnp.concatenate([lengths, swap(lengths, "row", bit)])
        bit *= 2
    return lengths


def exchange(blocks):
    return [blocks[0]] + [swap(blocks[k], "col", k) for k in range(1, len(blocks))]


def gather_cols(block):
    size = lax.axis_size("col")
    if size != 4:
        return [(block,)] + [(swap(block, "col", k),) for k in range(1, size)]
    near = swap(block, "col", 1)
    far = swap(block, "col", 2)
    middle = lax.ppermute(block, "col", [(1, 2), (2, 1)])
    ends = lax.ppermute(far, "col", [(2, 3), (1, 0)])
    return [(block,), (near,), (far,), (middle, ends)]


def collect(terms):
    size = lax.axis_size("col")
    if size != 4:
        parts = exchange(terms)
    else:
        ends = lax.ppermute(terms[3], "col", [(3, 2), (0, 1)])
        near = swap(terms[1], "col", 1)
        middle = lax.ppermute(terms[3], "col", [(1, 2), (2, 1)])
        both = terms[2].astype(jnp.float32) + ends.astype(jnp.float32)
        far = swap(both.astype(jnp.bfloat16), "col", 2)
        parts = [terms[0], near, far, middle]
    return sum(part.astype(jnp.float32) for part in parts)


def cut_kernel(cols, place, *refs):
    masters, outs = refs[:-cols], refs[-cols:]
    width = outs[0].shape[-1]
    for k in range(cols):
        target = lax.bitwise_xor(place[1], k)
        columns = pl.ds(pl.multiple_of(target * width, 128), width)
        if len(masters) == 1:
            outs[k][...] = masters[0][:, columns].astype(jnp.bfloat16)
        else:
            outs[k][0] = masters[0][:, columns].astype(jnp.bfloat16)
            outs[k][1] = masters[1][0, :, columns].astype(jnp.bfloat16)
            outs[k][2] = masters[1][1, :, columns].astype(jnp.bfloat16)


def cut(shape, place, *masters):
    cols = lax.axis_size("col")
    return pl.pallas_call(
        functools.partial(cut_kernel, cols),
        out_shape=[jax.ShapeDtypeStruct(shape, jnp.bfloat16)] * cols,
        in_specs=[SMEM] + [VMEM] * len(masters),
        out_specs=[VMEM] * cols,
        compiler_params=params(),
        cost_estimate=cost(0, 6 * math.prod(shape) * cols),
    )(place, *masters)


def turned(values):
    return values.astype(jnp.float32).T.astype(jnp.bfloat16)


def join_kernel(cols, kind, place, *refs):
    rows = refs[0].shape[-2]
    for k in range(cols):
        source = lax.bitwise_xor(place[1], k)
        where = pl.ds(pl.multiple_of(source * rows, 16), rows)
        if kind == "qkvg":
            refs[cols][where, :] = refs[k][...]
        elif kind == "out":
            refs[cols + 1][where, :] = refs[k][...]
        else:
            refs[cols + 2][where, :] = refs[k][0]
            refs[cols][0, where, :] = refs[k][1]
            refs[cols][1, where, :] = refs[k][2]
    if kind == "out":
        refs[cols][...] = turned(refs[cols + 1][...])
    elif kind == "feed":
        refs[cols + 1][...] = turned(refs[cols + 2][...])


def join(kind, blocks, place):
    cols = len(blocks)
    depth, width = blocks[0].shape[-2] * cols, blocks[0].shape[-1]
    shapes = {"qkvg": [(depth, width)], "out": [(width, depth)], "feed": [(2, depth, width), (width, depth)]}[kind]
    return pl.pallas_call(
        functools.partial(join_kernel, cols, kind),
        out_shape=[jax.ShapeDtypeStruct(shape, jnp.bfloat16) for shape in shapes],
        in_specs=[SMEM] + [VMEM] * cols,
        out_specs=[VMEM] * len(shapes),
        scratch_shapes=[] if kind == "qkvg" else [pltpu.VMEM((depth, width), jnp.bfloat16)],
        compiler_params=params(),
        cost_estimate=cost(0, 4 * math.prod(blocks[0].shape) * cols),
    )(place, *blocks)


def pack_kernel(requests, rows, passes, place, lengths, table, bins, starts, count, used):
    row = place[0]
    per_row = requests // rows

    def clear(i, carry):
        table[i] = -1
        return carry

    lax.fori_loop(0, passes * TILES, clear, 0)

    def clear_used(i, carry):
        used[i] = 0
        return carry

    lax.fori_loop(0, requests, clear_used, 0)

    def put(q, top):
        owner = q // per_row
        length = lengths[lax.bitwise_xor(owner, row) * per_row + (q - owner * per_row)]
        tiles = (length + (TILE - 1)) // TILE

        def look(i, best):
            b = requests - 1 - i
            return jnp.where(used[b] + tiles <= TILES, b, best)

        b = lax.fori_loop(0, requests, look, requests - 1)
        start = used[b]
        used[b] = start + tiles
        bins[q] = b
        starts[q] = start
        turn = b // rows

        @pl.when(b - turn * rows == row)
        def _():
            def note(i, carry):
                table[turn * TILES + start + i] = q * TILES + i
                return carry

            lax.fori_loop(0, tiles, note, 0)

        return jnp.maximum(top, b + 1)

    count[0] = lax.fori_loop(0, requests, put, 0)


def pack(place, lengths, rows):
    requests = lengths.shape[0]
    passes = requests // rows
    whole = lambda n: jax.ShapeDtypeStruct((n,), jnp.int32)
    return pl.pallas_call(
        functools.partial(pack_kernel, requests, rows, passes),
        out_shape=[whole(passes * TILES), whole(requests), whole(requests), whole(1)],
        in_specs=[SMEM, SMEM],
        out_specs=[SMEM] * 4,
        scratch_shapes=[pltpu.SMEM((requests,), jnp.int32)],
        compiler_params=params(),
    )(place, lengths)


def pick_kernel(rows, per_row, turn, place, table, *refs):
    pieces, out, sem = refs[:rows], refs[rows], refs[rows + 1]
    row = place[0]

    def step(i, carry):
        code = jnp.maximum(table[turn * TILES + i], 0)
        request = code // TILES
        owner = request // per_row
        tile = (request - owner * per_row) * TILES + (code - request * TILES)
        piece = lax.bitwise_xor(owner, row)
        source = pl.ds(pl.multiple_of(tile * TILE, TILE), TILE)
        target = pl.ds(pl.multiple_of(i * TILE, TILE), TILE)
        for j in range(rows):

            @pl.when(piece == j)
            def _():
                pltpu.make_async_copy(pieces[j].at[source, :], out.at[target, :], sem).start()

        return carry

    lax.fori_loop(0, TILES, step, 0)
    pltpu.make_async_copy(out, out, sem).wait()


def pick(place, table, pieces, turn):
    rows = len(pieces)
    width = pieces[0].shape[1]
    return pl.pallas_call(
        functools.partial(pick_kernel, rows, pieces[0].shape[0] // S, turn),
        out_shape=jax.ShapeDtypeStruct((S, width), jnp.bfloat16),
        in_specs=[SMEM, SMEM] + [ANY] * rows,
        out_specs=VMEM,
        scratch_shapes=[pltpu.SemaphoreType.DMA],
        compiler_params=params(),
        cost_estimate=cost(0, 4 * S * width),
    )(place, table, *pieces)


def spread_kernel(rows, per_row, total, place, lengths, bins, starts, *refs):
    pieces, out = refs[:total], refs[total]
    row = place[0]
    width = out.shape[1]
    for a in range(per_row):
        request = row * per_row + a
        length = lengths[a]
        b = bins[request]
        start = starts[request]
        turn = b // rows
        index = lax.bitwise_xor(b - turn * rows, row) + turn * rows
        tiles = (length + (TILE - 1)) // TILE

        def blank(i, carry):
            out[pl.ds(pl.multiple_of(a * S + i * TILE, TILE), TILE), :] = jnp.zeros((TILE, width), jnp.bfloat16)
            return carry

        lax.fori_loop(tiles, TILES, blank, 0)
        for j in range(total):

            @pl.when(index == j)
            def _():
                def move(i, carry):
                    values = pieces[j][pl.ds(pl.multiple_of((start + i) * TILE, TILE), TILE), :]
                    position = i * TILE + lax.broadcasted_iota(jnp.int32, (TILE, width), 0)
                    kept = jnp.where(position < length, values.astype(jnp.float32), 0.0)
                    out[pl.ds(pl.multiple_of(a * S + i * TILE, TILE), TILE), :] = kept.astype(jnp.bfloat16)
                    return carry

                lax.fori_loop(0, tiles, move, 0)


def spread(place, lengths, bins, starts, pieces, rows, per_row):
    width = pieces[0].shape[1]
    return pl.pallas_call(
        functools.partial(spread_kernel, rows, per_row, len(pieces)),
        out_shape=jax.ShapeDtypeStruct((per_row * S, width), jnp.bfloat16),
        in_specs=[SMEM] * 4 + [VMEM] * len(pieces),
        out_specs=VMEM,
        compiler_params=params(),
        cost_estimate=cost(0, 2 * S * width * (len(pieces) + per_row)),
    )(place, lengths, bins, starts, *pieces)


DOT = functools.partial(jnp.dot, preferred_element_type=jnp.float32)


def flatten(parts):
    return [part for entry in parts for part in entry], tuple(len(entry) for entry in parts)


def read_parts(refs, counts):
    at = 0
    for count in counts:
        block = refs[at][...]
        for other in refs[at + 1 : at + count]:
            block = block + other[...]
        at += count
        yield block


def silu(values):
    return values * (1.0 / (1.0 + jnp.exp(-values)))


def retain_kernel(rows, counts, heads, place, decays, cosine, sine, seg_col, seg_row, *refs):
    cols, number = len(counts), sum(counts)
    tokens, weights = refs[:number], refs[number : number + rows]
    mixed, normed, gathered, sems = refs[number + rows :]
    depth = D // rows
    width = D // cols
    parts = ((0, 2 * KEY), (2 * KEY, VAL), (2 * KEY + VAL, VAL))

    for head in range(heads):
        for i, (low, size) in enumerate(parts):
            columns = pl.ds(head * HEAD_WIDTH + low, size)
            for j in range(rows):
                where = pl.ds(pl.multiple_of(lax.bitwise_xor(place[0], j) * depth, depth), depth)
                pltpu.make_async_copy(
                    weights[j].at[:, columns], gathered.at[where, columns], sems.at[head * 3 + i]
                ).start()

    total = jnp.zeros((S, 1), jnp.float32)
    for block in read_parts(tokens, counts):
        values = block.astype(jnp.float32)
        total += jnp.sum(values * values, axis=1, keepdims=True)
    scale = lax.rsqrt(total / D + epsilon)
    for k, block in enumerate(read_parts(tokens, counts)):
        where = pl.ds(pl.multiple_of(lax.bitwise_xor(place[1], k) * width, width), width)
        normed[:, where] = (block.astype(jnp.float32) * scale).astype(jnp.bfloat16)

    def project(head, i):
        low, size = parts[i]
        columns = pl.ds(head * HEAD_WIDTH + low, size)
        view = gathered.at[:, columns]
        pltpu.make_async_copy(view, view, sems.at[head * 3 + i]).wait()
        return DOT(normed[...], gathered[:, columns]).astype(jnp.bfloat16)

    def rotate(values):
        values = values.astype(jnp.float32)
        first, second = values[:, : KEY // 2], values[:, KEY // 2 :]
        cos, sin = cosine[...], sine[...]
        return jnp.concatenate([first * cos - second * sin, first * sin + second * cos], axis=1)

    lag = lax.broadcasted_iota(jnp.int32, (S, S), 0) - lax.broadcasted_iota(jnp.int32, (S, S), 1)
    allowed = (lag >= 0) & (seg_col[...] == seg_row[...])
    span = jnp.where(allowed, lag.astype(jnp.float32), 1e6)
    for head in range(heads):
        both = project(head, 0)
        query = rotate(both[:, :KEY]).astype(jnp.bfloat16)
        keyed = (rotate(both[:, KEY:]) * (1.0 / math.sqrt(KEY))).astype(jnp.bfloat16)
        scores = lax.dot_general(query, keyed, (((1,), (1,)), ((), ())), preferred_element_type=jnp.float32)
        scores = scores * jnp.exp(span * decays[head])
        denom = jnp.sum(scores, axis=1, keepdims=True)
        value = project(head, 1)
        retained = DOT(scores.astype(jnp.bfloat16), value) / jnp.maximum(jnp.abs(denom), 1.0)
        centred = retained - jnp.mean(retained, axis=1, keepdims=True)
        spread_of = jnp.mean(centred * centred, axis=1, keepdims=True)
        grouped = centred * lax.rsqrt(spread_of + epsilon)
        gate = project(head, 2).astype(jnp.float32)
        mixed[:, head * VAL : (head + 1) * VAL] = (silu(gate) * grouped).astype(jnp.bfloat16)


def retain(place, decays, cosine, sine, seg_col, seg_row, tokens, weights):
    rows, cols = len(weights), len(tokens)
    heads = HEADS // cols
    flat, counts = flatten(tokens)
    return pl.pallas_call(
        functools.partial(retain_kernel, rows, counts, heads),
        out_shape=jax.ShapeDtypeStruct((S, heads * VAL), jnp.bfloat16),
        in_specs=[SMEM, SMEM] + [VMEM] * (4 + len(flat)) + [ANY] * rows,
        out_specs=VMEM,
        scratch_shapes=[
            pltpu.VMEM((S, D), jnp.bfloat16),
            pltpu.VMEM((D, heads * HEAD_WIDTH), jnp.bfloat16),
            pltpu.SemaphoreType.DMA((heads * 3,)),
        ],
        compiler_params=params(),
        cost_estimate=cost(2 * S * D * HEAD_WIDTH * heads * 1.3, 2 * D * HEAD_WIDTH * heads),
    )(place, decays, cosine, sine, seg_col, seg_row, *flat, *weights)


def load_terms(rows, cols, place, weights, gathered, sem):
    ratio = rows // cols
    for j in range(rows):
        owner = lax.bitwise_xor(place[0], j)
        target = owner // ratio
        slot = lax.bitwise_xor(target, place[1]) * ratio + (owner - target * ratio)
        pltpu.make_async_copy(weights[j], gathered.at[slot], sem).start()


def put_terms(rows, cols, left, gathered, sem, outs):
    ratio = rows // cols
    depth = D // rows
    pltpu.make_async_copy(gathered, gathered, sem).wait()
    for slot in range(rows):
        k, i = slot // ratio, slot % ratio
        outs[k][:, i * depth : (i + 1) * depth] = DOT(left, gathered[slot]).astype(jnp.bfloat16)


def mix_kernel(rows, cols, place, mixed, *refs):
    weights, outs = refs[:rows], refs[rows : rows + cols]
    gathered, sem = refs[rows + cols :]
    load_terms(rows, cols, place, weights, gathered, sem)
    put_terms(rows, cols, mixed[...], gathered, sem, outs)


def mix(place, mixed, weights, cols):
    rows = len(weights)
    width = D // cols
    return pl.pallas_call(
        functools.partial(mix_kernel, rows, cols),
        out_shape=[jax.ShapeDtypeStruct((S, width), jnp.bfloat16)] * cols,
        in_specs=[SMEM, VMEM] + [ANY] * rows,
        out_specs=[VMEM] * cols,
        scratch_shapes=[
            pltpu.VMEM((rows,) + weights[0].shape, jnp.bfloat16),
            pltpu.SemaphoreType.DMA,
        ],
        compiler_params=params(),
        cost_estimate=cost(2 * S * D * mixed.shape[1], 2 * D * mixed.shape[1]),
    )(place, mixed, *weights)


def feed_kernel(rows, counts, tile, place, *refs):
    cols, number = len(counts), sum(counts)
    tokens = refs[:number]
    pairs = refs[number : number + rows]
    downs = refs[number + rows : number + 2 * rows]
    outs = refs[number + 2 * rows : number + 2 * rows + cols]
    ordered, hidden, gathered, gathered_down, sems, sem_down = refs[number + 2 * rows + cols :]
    depth = D // rows
    width = D // cols
    steps = gathered.shape[2] // tile

    for step in range(steps):
        columns = pl.ds(step * tile, tile)
        for j in range(rows):
            where = pl.ds(pl.multiple_of(lax.bitwise_xor(place[0], j) * depth, depth), depth)
            pltpu.make_async_copy(
                pairs[j].at[:, :, columns], gathered.at[:, where, columns], sems.at[step]
            ).start()
    load_terms(rows, cols, place, downs, gathered_down, sem_down)

    total = jnp.zeros((S, 1), jnp.float32)
    for k, block in enumerate(read_parts(tokens, counts)):
        values = block.astype(jnp.float32)
        total += jnp.sum(values * values, axis=1, keepdims=True)
        where = pl.ds(pl.multiple_of(lax.bitwise_xor(place[1], k) * width, width), width)
        ordered[:, where] = block
    scale = lax.rsqrt(total / D + epsilon)

    for step in range(steps):
        columns = pl.ds(step * tile, tile)
        view = gathered.at[:, :, columns]
        pltpu.make_async_copy(view, view, sems.at[step]).wait()
        gate = DOT(ordered[...], gathered[0, :, columns]) * scale
        up = DOT(ordered[...], gathered[1, :, columns]) * scale
        hidden[:, columns] = (silu(gate) * up).astype(jnp.bfloat16)
    put_terms(rows, cols, hidden[...], gathered_down, sem_down, outs)


def feed(place, tokens, gateups, downs):
    rows, cols = len(gateups), len(tokens)
    units = gateups[0].shape[2]
    tile = min(units, 512)
    flat, counts = flatten(tokens)
    return pl.pallas_call(
        functools.partial(feed_kernel, rows, counts, tile),
        out_shape=[jax.ShapeDtypeStruct((S, D // cols), jnp.bfloat16)] * cols,
        in_specs=[SMEM] + [VMEM] * len(flat) + [ANY] * (2 * rows),
        out_specs=[VMEM] * cols,
        scratch_shapes=[
            pltpu.VMEM((S, D), jnp.bfloat16),
            pltpu.VMEM((S, units), jnp.bfloat16),
            pltpu.VMEM((2, D, units), jnp.bfloat16),
            pltpu.VMEM((rows,) + downs[0].shape, jnp.bfloat16),
            pltpu.SemaphoreType.DMA((units // tile,)),
            pltpu.SemaphoreType.DMA,
        ],
        compiler_params=params(),
        cost_estimate=cost(6 * S * D * units, 6 * D * units),
    )(place, *flat, *gateups, *downs)


def shards(hidden_states, lengths, qkvg_master, gateup_master, out_master, down_master):
    rows, cols = lax.axis_size("row"), lax.axis_size("col")
    per_row = lengths.shape[0]
    heads = HEADS // cols
    place = jnp.stack([lax.axis_index("row"), lax.axis_index("col")]).astype(jnp.int32)

    all_lengths = gather_lengths(lengths)
    depth = qkvg_master.shape[0]
    units = gateup_master.shape[2] // cols
    qkvg_parts = exchange(cut((depth, heads * HEAD_WIDTH), place, qkvg_master))
    everyone = gather_rows(after(hidden_states, all_lengths), behind=(qkvg_parts[1],))
    (qkvg_blocks,) = join("qkvg", qkvg_parts, place)
    out_cut = cut((depth, units), place, out_master.T)
    out_parts = exchange(list(after(tuple(out_cut), *qkvg_parts[1:])))
    (out_blocks,) = join("out", out_parts, place)

    table, bins, starts, count = pack(place, all_lengths, rows)

    head_ids = lax.axis_index("col") * heads + jnp.arange(heads)
    decays = jnp.log1p(-jnp.power(2.0, -5.0 - head_ids.astype(jnp.float32)))
    freq = jnp.power(10000.0, -2.0 * jnp.arange(KEY // 2).astype(jnp.float32) / KEY)

    def begin(turn):
        codes = table[turn * TILES : (turn + 1) * TILES]
        segments = jnp.where(codes < 0, -1, codes // TILES)
        seg = jnp.broadcast_to(segments[:, None], (TILES, TILE)).reshape(S)
        positions = ((jnp.maximum(codes, 0) % TILES)[:, None] * TILE + jnp.arange(TILE)[None, :]).reshape(S)
        angle = positions.astype(jnp.float32)[:, None] * freq[None, :]
        own = pick(place, table, everyone, turn)
        return own, (jnp.cos(angle), jnp.sin(angle), seg[:, None], seg[None, :])

    table = after(table, *out_parts[1:])
    own, tables = begin(0)
    tokens = gather_cols(own)
    qkvg_pieces = gather_rows(after(qkvg_blocks, *last_parts(everyone)), behind=[entry[0] for entry in tokens[1:]] + out_parts[1:])
    out_pieces = gather_rows(after(out_blocks, *last_parts(qkvg_pieces)), direct=True)

    feed_cut = cut((3, depth, units), place, down_master.T, gateup_master)
    behind = [part for entry in tokens[1:] for part in entry] + qkvg_pieces[1:]
    feed_parts = exchange(list(after(tuple(feed_cut), *behind)))

    mixed = retain(place, decays, *tables, tokens, qkvg_pieces)

    gateup_blocks, down_blocks = join("feed", list(after(tuple(feed_parts), mixed)), place)
    gateup_pieces = gather_rows(gateup_blocks)
    down_pieces = gather_rows(after(down_blocks, *last_parts(gateup_pieces)), direct=True)

    def layer(own, mixed):
        residual = own.astype(jnp.float32) + collect(mix(place, mixed, out_pieces, cols))
        terms = feed(place, gather_cols(residual.astype(jnp.bfloat16)), gateup_pieces, down_pieces)
        return gather_rows((residual + collect(terms)).astype(jnp.bfloat16), direct=True)

    first = layer(own, mixed)

    def finish(pieces):
        return spread(place, lengths, bins, starts, pieces, rows, per_row)

    def more(pieces):
        for turn in range(1, per_row):
            own, tables = begin(turn)
            pieces = pieces + layer(own, retain(place, decays, *tables, gather_cols(own), qkvg_pieces))
        return finish(pieces)

    layer_output = lax.cond(count[0] > rows, more, finish, first)
    return (layer_output, qkvg_blocks, gateup_blocks, out_blocks, down_blocks)


def solution(mesh):
    return jax.shard_map(
        shards,
        mesh=mesh,
        in_specs=(
            P("row", "col"),
            P("row"),
            P(("row", "col"), None),
            P(None, ("row", "col"), None),
            P(None, ("row", "col")),
            P(None, ("row", "col")),
        ),
        out_specs=(
            P("row", "col"),
            P("row", "col"),
            P(None, "row", "col"),
            P("col", "row"),
            P("col", "row"),
        ),
        check_vma=False,
    )
```

profile of v0, /device:TPU:0, one launch (start us, length us, event | category | flops | bytes accessed | tf_op | source)
XLA Modules:
  0.0 431.5 jit_solution(14458406472972612806)
XLA Ops:
  23.7 12.4 %collective-permute-done.35.refs_4_ = bf16[1024,512]{1,0:T(8,128)(2,1)S(1)} collective-permute-done((bf16[1024,512]{1,0:T(8,128)(2,1)}, bf16[1024,512]{1,0:T(8,128)(2,1)S(1)}, u32[]{:S(2)}, u32[]{:S(2)}) %collective-permute-start.35) | collective-permute-done | bytes 1048608 | tf_op jit(solution)/shard_map/ppermute | solution.py:38
  37.6 3.7 collective-permute-start.28
  43.7 7.7 %collective-permute-done.28.refs_3_ = bf16[64,3072]{1,0:T(8,128)(2,1)} collective-permute-done((bf16[64,3072]{1,0:T(8,128)(2,1)}, bf16[64,3072]{1,0:T(8,128)(2,1)}, u32[]{:S(2)}, u32[]{:S(2)}) %collective-permute-start.28) | collective-permute-done | bytes 393248 | tf_op jit(solution)/shard_map/ppermute | solution.py:38
  55.4 9.8 %collective-permute-done.38 = bf16[512,512]{1,0:T(8,128)(2,1)} collective-permute-done((bf16[512,512]{1,0:T(8,128)(2,1)}, bf16[512,512]{1,0:T(8,128)(2,1)}, u32[]{:S(2)}, u32[]{:S(2)}) %collective-permute-start.38) | collective-permute-done | bytes 524320 | tf_op jit(solution)/shard_map/ppermute | solution.py:38
  70.3 8.0 %collective-permute-start.29 = (bf16[64,1024]{1,0:T(8,128)(2,1)}, bf16[64,1024]{1,0:T(8,128)(2,1)S(1)}, u32[]{:S(2)}, u32[]{:S(2)}) collective-permute-start(bf16[64,1024]{1,0:T(8,128)(2,1)} %get-tuple-element.281), channel_id=1, source_target_pairs={{0,1},{1,0},{2,3},{3,2},{4,5},{5,4},{6,7},{7,6},{8,9},{9,8},{10,11... | collective-permute-start | bytes 393224 | tf_op jit(solution)/shard_map/ppermute | solution.py:38
  79.4 4.9 %collective-permute-done.29.refs_1_ = bf16[64,1024]{1,0:T(8,128)(2,1)S(1)} collective-permute-done((bf16[64,1024]{1,0:T(8,128)(2,1)}, bf16[64,1024]{1,0:T(8,128)(2,1)S(1)}, u32[]{:S(2)}, u32[]{:S(2)}) %collective-permute-start.29) | collective-permute-done | bytes 131104 | tf_op jit(solution)/shard_map/ppermute | solution.py:38
  85.7 4.1 shard_map.101
  91.3 4.0 shard_map.104.refs_0_
  96.1 5.0 %collective-permute-start.41 = (bf16[512,512]{1,0:T(8,128)(2,1)}, bf16[512,512]{1,0:T(8,128)(2,1)}, u32[]{:S(2)}, u32[]{:S(2)}) collective-permute-start(bf16[512,512]{1,0:T(8,128)(2,1)} %shard_map.104.refs_0_), channel_id=1, source_target_pairs={{0,2},{1,3},{2,0},{3,1},{4,6},{5,7},{6,4},{7,5},{8,10},{9,11},{10,... | collective-permute-start | bytes 1572872 | tf_op jit(solution)/shard_map/ppermute | solution.py:38
  101.3 34.3 %collective-permute-done.41.refs_2_ = bf16[512,512]{1,0:T(8,128)(2,1)} collective-permute-done((bf16[512,512]{1,0:T(8,128)(2,1)}, bf16[512,512]{1,0:T(8,128)(2,1)}, u32[]{:S(2)}, u32[]{:S(2)}) %collective-permute-start.41) | collective-permute-done | bytes 524320 | tf_op jit(solution)/shard_map/ppermute | solution.py:38
  141.8 14.4 %collective-permute-done.49 = bf16[128,3072]{1,0:T(8,128)(2,1)S(1)} collective-permute-done((bf16[128,3072]{1,0:T(8,128)(2,1)S(1)}, bf16[128,3072]{1,0:T(8,128)(2,1)S(1)}, u32[]{:S(2)}, u32[]{:S(2)}) %collective-permute-start.49) | collective-permute-done | bytes 786464 | tf_op jit(solution)/shard_map/ppermute | solution.py:38
  173.7 7.9 %collective-permute-done.43.refs_4_ = bf16[512,512]{1,0:T(8,128)(2,1)} collective-permute-done((bf16[512,512]{1,0:T(8,128)(2,1)}, bf16[512,512]{1,0:T(8,128)(2,1)}, u32[]{:S(2)}, u32[]{:S(2)}) %collective-permute-start.43) | collective-permute-done | bytes 524320 | tf_op jit(solution)/shard_map/ppermute | solution.py:94
  182.6 10.8 %collective-permute-done.55.refs_4_ = bf16[1024,256]{1,0:T(8,128)(2,1)} collective-permute-done((bf16[1024,256]{1,0:T(8,128)(2,1)}, bf16[1024,256]{1,0:T(8,128)(2,1)}, u32[]{:S(2)}, u32[]{:S(2)}) %collective-permute-start.55) | collective-permute-done | bytes 524320 | tf_op jit(solution)/shard_map/ppermute | solution.py:38
  197.0 15.1 %shard_map.106.mixed = bf16[512,1024]{1,0:T(8,128)(2,1)} custom-call(s32[2]{0:T(128)S(1)} %pad_add_fusion.place, f32[2]{0:T(128)S(1)} %negate_log-plus-one_fusion.decays, f32[512,128]{1,0:T(8,128)} %get-tuple-element.322.cosine, f32[512,128]{1,0:T(8,128)} %get-tuple-element.321.sine, s32[512,1]{1,0:T(8,128)} %broadcast_in_dim_reshape.8.seg_col, ...), custom_call_target="tpu_custom_call" | custom-call | flops 8375186432 | bytes 12582912 | tf_op jit(solution)/shard_map/pallas_call | solution.py:400
  214.7 6.3 %shard_map.108 = (bf16[512,512]{1,0:T(8,128)(2,1)}, bf16[512,512]{1,0:T(8,128)(2,1)}, bf16[512,512]{1,0:T(8,128)(2,1)}, bf16[512,512]{1,0:T(8,128)(2,1)}) custom-call(s32[2]{0:T(128)S(1)} %pad_add_fusion.place, bf16[512,1024]{1,0:T(8,128)(2,1)} %shard_map.106.mixed, bf16[1024,256]{1,0:T(8,128)(2,1)} %shard_map.107.refs_0_, ...), custom_call_target="tpu_custom_call" | custom-call | flops 2147483648 | bytes 4194304 | tf_op jit(solution)/shard_map/pallas_call | solution.py:443
  224.3 16.4 %collective-permute-done.68.refs_2_ = bf16[3,64,1024]{2,1,0:T(8,128)(2,1)S(1)} collective-permute-done((bf16[3,64,1024]{2,1,0:T(8,128)(2,1)S(1)}, bf16[3,64,1024]{2,1,0:T(8,128)(2,1)S(1)}, u32[]{:S(2)}, u32[]{:S(2)}) %collective-permute-start.68) | collective-permute-done | bytes 393248 | tf_op jit(solution)/shard_map/ppermute | solution.py:38
  247.1 8.1 %collective-permute-start.59 = (bf16[512,512]{1,0:T(8,128)(2,1)}, bf16[512,512]{1,0:T(8,128)(2,1)S(1)}, u32[]{:S(2)}, u32[]{:S(2)}) collective-permute-start(bf16[512,512]{1,0:T(8,128)(2,1)} %get-tuple-element.295), channel_id=1, source_target_pairs={{0,1},{1,0},{2,3},{3,2},{4,5},{5,4},{6,7},{7,6},{8,9},{9,8},{10,11... | collective-permute-start | bytes 1572872 | tf_op jit(solution)/shard_map/ppermute | solution.py:38
  256.4 10.6 %collective-permute-done.59 = bf16[512,512]{1,0:T(8,128)(2,1)S(1)} collective-permute-done((bf16[512,512]{1,0:T(8,128)(2,1)}, bf16[512,512]{1,0:T(8,128)(2,1)S(1)}, u32[]{:S(2)}, u32[]{:S(2)}) %collective-permute-start.59) | collective-permute-done | bytes 524320 | tf_op jit(solution)/shard_map/ppermute | solution.py:38
  272.1 20.1 %collective-permute-done.61 = bf16[512,512]{1,0:T(8,128)(2,1)S(1)} collective-permute-done((bf16[512,512]{1,0:T(8,128)(2,1)S(1)}, bf16[512,512]{1,0:T(8,128)(2,1)S(1)}, u32[]{:S(2)}, u32[]{:S(2)}) %collective-permute-start.61) | collective-permute-done | bytes 524320 | tf_op jit(solution)/shard_map/ppermute | solution.py:38
  294.1 11.6 %collective-permute-done.76 = bf16[1,256,1024]{2,1,0:T(8,128)(2,1)S(1)} collective-permute-done((bf16[1,256,1024]{2,1,0:T(8,128)(2,1)S(1)}, bf16[1,256,1024]{2,1,0:T(8,128)(2,1)S(1)}, u32[]{:S(2)}, u32[]{:S(2)}) %collective-permute-start.76) | collective-permute-done | bytes 524320 | tf_op jit(solution)/shard_map/ppermute | solution.py:38
  305.8 11.5 %collective-permute-done.64.refs_2_ = bf16[512,512]{1,0:T(8,128)(2,1)S(1)} collective-permute-done((bf16[512,512]{1,0:T(8,128)(2,1)S(1)}, bf16[512,512]{1,0:T(8,128)(2,1)S(1)}, u32[]{:S(2)}, u32[]{:S(2)}) %collective-permute-start.64) | collective-permute-done | bytes 524320 | tf_op jit(solution)/shard_map/ppermute | solution.py:38
  321.8 6.7 %collective-permute-done.63.refs_1_ = bf16[512,512]{1,0:T(8,128)(2,1)} collective-permute-done((bf16[512,512]{1,0:T(8,128)(2,1)S(1)}, bf16[512,512]{1,0:T(8,128)(2,1)}, u32[]{:S(2)}, u32[]{:S(2)}) %collective-permute-start.63) | collective-permute-done | bytes 524320 | tf_op jit(solution)/shard_map/ppermute | solution.py:38
  330.2 9.4 %collective-permute-done.66.refs_4_ = bf16[512,512]{1,0:T(8,128)(2,1)S(1)} collective-permute-done((bf16[512,512]{1,0:T(8,128)(2,1)S(1)}, bf16[512,512]{1,0:T(8,128)(2,1)S(1)}, u32[]{:S(2)}, u32[]{:S(2)}) %collective-permute-start.66) | collective-permute-done | bytes 524320 | tf_op jit(solution)/shard_map/ppermute | solution.py:94
  340.4 4.7 %collective-permute-done.81.refs_17_ = bf16[1024,256]{1,0:T(8,128)(2,1)S(1)} collective-permute-done((bf16[1024,256]{1,0:T(8,128)(2,1)S(1)}, bf16[1024,256]{1,0:T(8,128)(2,1)S(1)}, u32[]{:S(2)}, u32[]{:S(2)}) %collective-permute-start.81) | collective-permute-done | bytes 524320 | tf_op jit(solution)/shard_map/ppermute | solution.py:38
  348.0 11.6 %shard_map.111 = (bf16[512,512]{1,0:T(8,128)(2,1)}, bf16[512,512]{1,0:T(8,128)(2,1)}, bf16[512,512]{1,0:T(8,128)(2,1)}, bf16[512,512]{1,0:T(8,128)(2,1)}) custom-call(s32[2]{0:T(128)S(1)} %pad_add_fusion.place, bf16[512,512]{1,0:T(8,128)(2,1)} %copy-done.35, bf16[512,512]{1,0:T(8,128)(2,1)} %collective-permute-done.63.refs_1_, bf16[512,512]{1,0:T(8,128)(2,1)} %copy-done.76, ...), custom_call_target="tpu_custom_call" | custom-call | flops 6442450944 | bytes 12582912 | tf_op jit(solution)/shard_map/pallas_call | solution.py:500
  359.6 4.7 %collective-permute-start.86 = (bf16[512,512]{1,0:T(8,128)(2,1)}, bf16[512,512]{1,0:T(8,128)(2,1)S(1)}, u32[]{:S(2)}, u32[]{:S(2)}) collective-permute-start(bf16[512,512]{1,0:T(8,128)(2,1)} %get-tuple-element.316), channel_id=1, source_target_pairs={{3,2},{0,1},{7,6},{4,5},{11,10},{8,9},{15,14},{12,13},{19,18},{16,... | collective-permute-start | bytes 1572872 | tf_op jit(solution)/shard_map/ppermute | solution.py:103
  367.4 9.5 %collective-permute-done.86 = bf16[512,512]{1,0:T(8,128)(2,1)S(1)} collective-permute-done((bf16[512,512]{1,0:T(8,128)(2,1)}, bf16[512,512]{1,0:T(8,128)(2,1)S(1)}, u32[]{:S(2)}, u32[]{:S(2)}) %collective-permute-start.86) | collective-permute-done | bytes 524320 | tf_op jit(solution)/shard_map/ppermute | solution.py:103
  378.1 3.6 collective-permute-start.87
  381.7 6.5 %collective-permute-done.85 = bf16[512,512]{1,0:T(8,128)(2,1)S(1)} collective-permute-done((bf16[512,512]{1,0:T(8,128)(2,1)}, bf16[512,512]{1,0:T(8,128)(2,1)S(1)}, u32[]{:S(2)}, u32[]{:S(2)}) %collective-permute-start.85) | collective-permute-done | bytes 524320 | tf_op jit(solution)/shard_map/ppermute | solution.py:38
  388.2 15.4 %collective-permute-done.87 = bf16[512,512]{1,0:T(8,128)(2,1)S(1)} collective-permute-done((bf16[512,512]{1,0:T(8,128)(2,1)S(1)}, bf16[512,512]{1,0:T(8,128)(2,1)S(1)}, u32[]{:S(2)}, u32[]{:S(2)}) %collective-permute-start.87) | collective-permute-done | bytes 524320 | tf_op jit(solution)/shard_map/ppermute | solution.py:38
  407.7 11.3 %collective-permute-done.94 = bf16[512,512]{1,0:T(8,128)(2,1)S(1)} collective-permute-done((bf16[512,512]{1,0:T(8,128)(2,1)S(1)}, bf16[512,512]{1,0:T(8,128)(2,1)S(1)}, u32[]{:S(2)}, u32[]{:S(2)}) %collective-permute-start.94) | collective-permute-done | bytes 524320 | tf_op jit(solution)/shard_map/ppermute | solution.py:38
  419.0 5.5 %collective-permute-done.92 = bf16[512,512]{1,0:T(8,128)(2,1)S(1)} collective-permute-done((bf16[512,512]{1,0:T(8,128)(2,1)S(1)}, bf16[512,512]{1,0:T(8,128)(2,1)S(1)}, u32[]{:S(2)}, u32[]{:S(2)}) %collective-permute-start.92) | collective-permute-done | bytes 524320 | tf_op jit(solution)/shard_map/ppermute | solution.py:38
  (245 shorter events, 114.5 us)
Async XLA Ops:
  23.7 42.7 %collective-permute-start.32 = (bf16[1024,512]{1,0:T(8,128)(2,1)S(1)}, bf16[1024,512]{1,0:T(8,128)(2,1)S(1)}, u32[]{:S(2)}, u32[]{:S(2)}) collective-permute-start(bf16[1024,512]{1,0:T(8,128)(2,1)S(1)} %copy-done.4), channel_id=1, source_target_pairs={{0,4},{4,0},{8,12},{12,8},{16,20},{20,16},{24,28},{28,24},{1,5},{5... | collective-permute-start | bytes 3145736 | tf_op jit(solution)/shard_map/ppermute | solution.py:38
  36.1 30.3 %collective-permute-start.36 = (bf16[1024,512]{1,0:T(8,128)(2,1)S(1)}, bf16[1024,512]{1,0:T(8,128)(2,1)S(1)}, u32[]{:S(2)}, u32[]{:S(2)}) collective-permute-start(bf16[1024,512]{1,0:T(8,128)(2,1)S(1)} %collective-permute-done.35.refs_4_), channel_id=1, source_target_pairs={{0,4},{4,0},{8,12},{12,8},{16,20},{20,16},{24,28},{28,24},{1,5},{5... | collective-permute-start | bytes 3145736 | tf_op jit(solution)/shard_map/ppermute | solution.py:38
  37.6 28.8 %collective-permute-start.34 = (bf16[1024,512]{1,0:T(8,128)(2,1)S(1)}, bf16[1024,512]{1,0:T(8,128)(2,1)S(1)}, u32[]{:S(2)}, u32[]{:S(2)}) collective-permute-start(bf16[1024,512]{1,0:T(8,128)(2,1)S(1)} %collective-permute-done.33.refs_2_), channel_id=1, source_target_pairs={{0,4},{4,0},{8,12},{12,8},{16,20},{20,16},{24,28},{28,24},{1,5},{5... | collective-permute-start | bytes 3145736 | tf_op jit(solution)/shard_map/ppermute | solution.py:38
  66.3 25.1 %collective-permute-start.39 = (bf16[1024,512]{1,0:T(8,128)(2,1)S(1)}, bf16[1024,512]{1,0:T(8,128)(2,1)}, u32[]{:S(2)}, u32[]{:S(2)}) collective-permute-start(bf16[1024,512]{1,0:T(8,128)(2,1)S(1)} %constant_dynamic-update-slice_fusion.refs_6_), channel_id=1, source_target_pairs={{0,4},{4,0},{8,12},{12,8},{16,20},{20,16},{24,28},{28,24},{1,5},{5... | collective-permute-start | bytes 3145736 | tf_op jit(solution)/shard_map/ppermute | solution.py:38
  66.4 69.2 %collective-permute-start.47 = (bf16[256,3072]{1,0:T(8,128)(2,1)}, bf16[256,3072]{1,0:T(8,128)(2,1)}, u32[]{:S(2)}, u32[]{:S(2)}) collective-permute-start(bf16[256,3072]{1,0:T(8,128)(2,1)} %shard_map.105.refs_5_), channel_id=1, source_target_pairs={{0,16},{4,20},{8,24},{12,28},{16,0},{20,4},{24,8},{28,12},{1,17},{... | collective-permute-start | bytes 4718600 | tf_op jit(solution)/shard_map/ppermute | solution.py:38
  66.8 69.6 %collective-permute-start.45 = (bf16[256,3072]{1,0:T(8,128)(2,1)}, bf16[256,3072]{1,0:T(8,128)(2,1)}, u32[]{:S(2)}, u32[]{:S(2)}) collective-permute-start(bf16[256,3072]{1,0:T(8,128)(2,1)} %shard_map.105.refs_5_), channel_id=1, source_target_pairs={{0,8},{4,12},{8,0},{12,4},{16,24},{20,28},{24,16},{28,20},{1,9},{5... | collective-permute-start | bytes 4718600 | tf_op jit(solution)/shard_map/ppermute | solution.py:38
  96.1 39.4 %collective-permute-start.41 = (bf16[512,512]{1,0:T(8,128)(2,1)}, bf16[512,512]{1,0:T(8,128)(2,1)}, u32[]{:S(2)}, u32[]{:S(2)}) collective-permute-start(bf16[512,512]{1,0:T(8,128)(2,1)} %shard_map.104.refs_0_), channel_id=1, source_target_pairs={{0,2},{1,3},{2,0},{3,1},{4,6},{5,7},{6,4},{7,5},{8,10},{9,11},{10,... | collective-permute-start | bytes 1572872 | tf_op jit(solution)/shard_map/ppermute | solution.py:38
  101.2 34.4 %collective-permute-start.40 = (bf16[512,512]{1,0:T(8,128)(2,1)}, bf16[512,512]{1,0:T(8,128)(2,1)S(1)}, u32[]{:S(2)}, u32[]{:S(2)}) collective-permute-start(bf16[512,512]{1,0:T(8,128)(2,1)} %shard_map.104.refs_0_), channel_id=1, source_target_pairs={{0,1},{1,0},{2,3},{3,2},{4,5},{5,4},{6,7},{7,6},{8,9},{9,8},{10,11... | collective-permute-start | bytes 1572872 | tf_op jit(solution)/shard_map/ppermute | solution.py:38
  141.2 25.2 %collective-permute-start.44 = (bf16[256,3072]{1,0:T(8,128)(2,1)}, bf16[256,3072]{1,0:T(8,128)(2,1)}, u32[]{:S(2)}, u32[]{:S(2)}) collective-permute-start(bf16[256,3072]{1,0:T(8,128)(2,1)} %shard_map.105.refs_5_), channel_id=1, source_target_pairs={{0,4},{4,0},{8,12},{12,8},{16,20},{20,16},{24,28},{28,24},{1,5},{5... | collective-permute-start | bytes 4718600 | tf_op jit(solution)/shard_map/ppermute | solution.py:38
  141.2 25.2 %collective-permute-start.48 = (bf16[256,3072]{1,0:T(8,128)(2,1)}, bf16[256,3072]{1,0:T(8,128)(2,1)}, u32[]{:S(2)}, u32[]{:S(2)}) collective-permute-start(bf16[256,3072]{1,0:T(8,128)(2,1)} %collective-permute-done.47.refs_9_), channel_id=1, source_target_pairs={{0,4},{4,0},{8,12},{12,8},{16,20},{20,16},{24,28},{28,24},{1,5},{5... | collective-permute-start | bytes 4718600 | tf_op jit(solution)/shard_map/ppermute | solution.py:38
  141.8 24.7 %collective-permute-start.46 = (bf16[256,3072]{1,0:T(8,128)(2,1)}, bf16[256,3072]{1,0:T(8,128)(2,1)}, u32[]{:S(2)}, u32[]{:S(2)}) collective-permute-start(bf16[256,3072]{1,0:T(8,128)(2,1)} %collective-permute-done.45.refs_7_), channel_id=1, source_target_pairs={{0,4},{4,0},{8,12},{12,8},{16,20},{20,16},{24,28},{28,24},{1,5},{5... | collective-permute-start | bytes 4718600 | tf_op jit(solution)/shard_map/ppermute | solution.py:38
  159.6 34.3 %collective-permute-start.51 = (bf16[256,3072]{1,0:T(8,128)(2,1)}, bf16[256,3072]{1,0:T(8,128)(2,1)}, u32[]{:S(2)}, u32[]{:S(2)}) collective-permute-start(bf16[256,3072]{1,0:T(8,128)(2,1)} %constant_dynamic-update-slice_fusion.2.refs_11_), channel_id=1, source_target_pairs={{0,4},{4,0},{8,12},{12,8},{16,20},{20,16},{24,28},{28,24},{1,5},{5... | collective-permute-start | bytes 4718600 | tf_op jit(solution)/shard_map/ppermute | solution.py:38
  168.2 25.2 %collective-permute-start.55 = (bf16[1024,256]{1,0:T(8,128)(2,1)}, bf16[1024,256]{1,0:T(8,128)(2,1)}, u32[]{:S(2)}, u32[]{:S(2)}) collective-permute-start(bf16[1024,256]{1,0:T(8,128)(2,1)} %shard_map.107.refs_0_), channel_id=1, source_target_pairs={{0,16},{4,20},{8,24},{12,28},{16,0},{20,4},{24,8},{28,12},{1,17},{... | collective-permute-start | bytes 1572872 | tf_op jit(solution)/shard_map/ppermute | solution.py:38
  168.5 24.9 %collective-permute-start.53 = (bf16[1024,256]{1,0:T(8,128)(2,1)}, bf16[1024,256]{1,0:T(8,128)(2,1)}, u32[]{:S(2)}, u32[]{:S(2)}) collective-permute-start(bf16[1024,256]{1,0:T(8,128)(2,1)} %shard_map.107.refs_0_), channel_id=1, source_target_pairs={{0,8},{4,12},{8,0},{12,4},{16,24},{20,28},{24,16},{28,20},{1,9},{5... | collective-permute-start | bytes 1572872 | tf_op jit(solution)/shard_map/ppermute | solution.py:38
  181.6 30.6 %collective-permute-start.52 = (bf16[1024,256]{1,0:T(8,128)(2,1)}, bf16[1024,256]{1,0:T(8,128)(2,1)S(1)}, u32[]{:S(2)}, u32[]{:S(2)}) collective-permute-start(bf16[1024,256]{1,0:T(8,128)(2,1)} %shard_map.107.refs_0_), channel_id=1, source_target_pairs={{0,4},{4,0},{8,12},{12,8},{16,20},{20,16},{24,28},{28,24},{1,5},{5... | collective-permute-start | bytes 1572872 | tf_op jit(solution)/shard_map/ppermute | solution.py:38
  182.6 29.7 %collective-permute-start.58 = (bf16[1024,256]{1,0:T(8,128)(2,1)}, bf16[1024,256]{1,0:T(8,128)(2,1)S(1)}, u32[]{:S(2)}, u32[]{:S(2)}) collective-permute-start(bf16[1024,256]{1,0:T(8,128)(2,1)} %collective-permute-done.57.refs_6_), channel_id=1, source_target_pairs={{0,4},{4,0},{8,12},{12,8},{16,20},{20,16},{24,28},{28,24},{1,5},{5... | collective-permute-start | bytes 1572872 | tf_op jit(solution)/shard_map/ppermute | solution.py:38
  193.9 30.4 %collective-permute-start.67 = (bf16[3,64,1024]{2,1,0:T(8,128)(2,1)}, bf16[3,64,1024]{2,1,0:T(8,128)(2,1)S(1)}, u32[]{:S(2)}, u32[]{:S(2)}) collective-permute-start(bf16[3,64,1024]{2,1,0:T(8,128)(2,1)} %get-tuple-element.303), channel_id=1, source_target_pairs={{0,1},{1,0},{2,3},{3,2},{4,5},{5,4},{6,7},{7,6},{8,9},{9,8},{10,11... | collective-permute-start | bytes 1179656 | tf_op jit(solution)/shard_map/ppermute | solution.py:38
  212.1 28.5 %collective-permute-start.68 = (bf16[3,64,1024]{2,1,0:T(8,128)(2,1)S(1)}, bf16[3,64,1024]{2,1,0:T(8,128)(2,1)S(1)}, u32[]{:S(2)}, u32[]{:S(2)}) collective-permute-start(bf16[3,64,1024]{2,1,0:T(8,128)(2,1)S(1)} %copy-done.89), channel_id=1, source_target_pairs={{0,2},{1,3},{2,0},{3,1},{4,6},{5,7},{6,4},{7,5},{8,10},{9,11},{10,... | collective-permute-start | bytes 1179656 | tf_op jit(solution)/shard_map/ppermute | solution.py:38
  212.3 28.4 %collective-permute-start.69 = (bf16[3,64,1024]{2,1,0:T(8,128)(2,1)S(1)}, bf16[3,64,1024]{2,1,0:T(8,128)(2,1)S(1)}, u32[]{:S(2)}, u32[]{:S(2)}) collective-permute-start(bf16[3,64,1024]{2,1,0:T(8,128)(2,1)S(1)} %copy-done.88), channel_id=1, source_target_pairs={{0,3},{1,2},{2,1},{3,0},{4,7},{5,6},{6,5},{7,4},{8,11},{9,10},{10,... | collective-permute-start | bytes 1179656 | tf_op jit(solution)/shard_map/ppermute | solution.py:38
  221.1 35.1 %collective-permute-start.60 = (bf16[512,512]{1,0:T(8,128)(2,1)}, bf16[512,512]{1,0:T(8,128)(2,1)S(1)}, u32[]{:S(2)}, u32[]{:S(2)}) collective-permute-start(bf16[512,512]{1,0:T(8,128)(2,1)} %get-tuple-element.297), channel_id=1, source_target_pairs={{3,2},{0,1},{7,6},{4,5},{11,10},{8,9},{15,14},{12,13},{19,18},{16,... | collective-permute-start | bytes 1572872 | tf_op jit(solution)/shard_map/ppermute | solution.py:103
  244.9 25.2 %collective-permute-start.73 = (bf16[2,256,1024]{2,1,0:T(8,128)(2,1)}, bf16[2,256,1024]{2,1,0:T(8,128)(2,1)S(1)}, u32[]{:S(2)}, u32[]{:S(2)}) collective-permute-start(bf16[2,256,1024]{2,1,0:T(8,128)(2,1)} %get-tuple-element.267.refs_5_), channel_id=1, source_target_pairs={{0,16},{4,20},{8,24},{12,28},{16,0},{20,4},{24,8},{28,12},{1,17},{... | collective-permute-start | bytes 3145736 | tf_op jit(solution)/shard_map/ppermute | solution.py:38
  245.7 24.9 %collective-permute-start.71 = (bf16[2,256,1024]{2,1,0:T(8,128)(2,1)}, bf16[2,256,1024]{2,1,0:T(8,128)(2,1)S(1)}, u32[]{:S(2)}, u32[]{:S(2)}) collective-permute-start(bf16[2,256,1024]{2,1,0:T(8,128)(2,1)} %get-tuple-element.267.refs_5_), channel_id=1, source_target_pairs={{0,8},{4,12},{8,0},{12,4},{16,24},{20,28},{24,16},{28,20},{1,9},{5... | collective-permute-start | bytes 3145736 | tf_op jit(solution)/shard_map/ppermute | solution.py:38
  256.1 37.1 %collective-permute-start.70 = (bf16[2,256,1024]{2,1,0:T(8,128)(2,1)}, bf16[2,256,1024]{2,1,0:T(8,128)(2,1)S(1)}, u32[]{:S(2)}, u32[]{:S(2)}) collective-permute-start(bf16[2,256,1024]{2,1,0:T(8,128)(2,1)} %get-tuple-element.267.refs_5_), channel_id=1, source_target_pairs={{0,4},{4,0},{8,12},{12,8},{16,20},{20,16},{24,28},{28,24},{1,5},{5... | collective-permute-start | bytes 3145736 | tf_op jit(solution)/shard_map/ppermute | solution.py:38
  267.0 25.3 %collective-permute-start.61 = (bf16[512,512]{1,0:T(8,128)(2,1)S(1)}, bf16[512,512]{1,0:T(8,128)(2,1)S(1)}, u32[]{:S(2)}, u32[]{:S(2)}) collective-permute-start(bf16[512,512]{1,0:T(8,128)(2,1)S(1)} %add_convert_fusion.6), channel_id=1, source_target_pairs={{0,2},{1,3},{2,0},{3,1},{4,6},{5,7},{6,4},{7,5},{8,10},{9,11},{10,... | collective-permute-start | bytes 1572872 | tf_op jit(solution)/shard_map/ppermute | solution.py:38
  270.1 48.4 %collective-permute-start.74 = (bf16[2,256,1024]{2,1,0:T(8,128)(2,1)S(1)}, bf16[2,256,1024]{2,1,0:T(8,128)(2,1)S(1)}, u32[]{:S(2)}, u32[]{:S(2)}) collective-permute-start(bf16[2,256,1024]{2,1,0:T(8,128)(2,1)S(1)} %collective-permute-done.73.refs_9_), channel_id=1, source_target_pairs={{0,4},{4,0},{8,12},{12,8},{16,20},{20,16},{24,28},{28,24},{1,5},{5... | collective-permute-start | bytes 3145736 | tf_op jit(solution)/shard_map/ppermute | solution.py:38
  270.6 48.1 %collective-permute-start.72 = (bf16[2,256,1024]{2,1,0:T(8,128)(2,1)S(1)}, bf16[2,256,1024]{2,1,0:T(8,128)(2,1)S(1)}, u32[]{:S(2)}, u32[]{:S(2)}) collective-permute-start(bf16[2,256,1024]{2,1,0:T(8,128)(2,1)S(1)} %collective-permute-done.71.refs_7_), channel_id=1, source_target_pairs={{0,4},{4,0},{8,12},{12,8},{16,20},{20,16},{24,28},{28,24},{1,5},{5... | collective-permute-start | bytes 3145736 | tf_op jit(solution)/shard_map/ppermute | solution.py:38
  293.2 24.1 %collective-permute-start.64 = (bf16[512,512]{1,0:T(8,128)(2,1)S(1)}, bf16[512,512]{1,0:T(8,128)(2,1)S(1)}, u32[]{:S(2)}, u32[]{:S(2)}) collective-permute-start(bf16[512,512]{1,0:T(8,128)(2,1)S(1)} %fusion.3.refs_0_), channel_id=1, source_target_pairs={{0,2},{1,3},{2,0},{3,1},{4,6},{5,7},{6,4},{7,5},{8,10},{9,11},{10,... | collective-permute-start | bytes 1572872 | tf_op jit(solution)/shard_map/ppermute | solution.py:38
  293.3 27.3 %collective-permute-start.65 = (bf16[512,512]{1,0:T(8,128)(2,1)S(1)}, bf16[512,512]{1,0:T(8,128)(2,1)S(1)}, u32[]{:S(2)}, u32[]{:S(2)}) collective-permute-start(bf16[512,512]{1,0:T(8,128)(2,1)S(1)} %fusion.3.refs_0_), channel_id=1, source_target_pairs={{1,2},{2,1},{5,6},{6,5},{9,10},{10,9},{13,14},{14,13},{17,18},{18,... | collective-permute-start | bytes 1572872 | tf_op jit(solution)/shard_map/ppermute | solution.py:93
  318.6 27.1 %collective-permute-start.77 = (bf16[2,256,1024]{2,1,0:T(8,128)(2,1)S(1)}, bf16[2,256,1024]{2,1,0:T(8,128)(2,1)S(1)}, u32[]{:S(2)}, u32[]{:S(2)}) collective-permute-start(bf16[2,256,1024]{2,1,0:T(8,128)(2,1)S(1)} %constant_dynamic-update-slice_fusion.4.refs_11_), channel_id=1, source_target_pairs={{0,4},{4,0},{8,12},{12,8},{16,20},{20,16},{24,28},{28,24},{1,5},{5... | collective-permute-start | bytes 3145736 | tf_op jit(solution)/shard_map/ppermute | solution.py:38
  320.6 24.6 %collective-permute-start.81 = (bf16[1024,256]{1,0:T(8,128)(2,1)S(1)}, bf16[1024,256]{1,0:T(8,128)(2,1)S(1)}, u32[]{:S(2)}, u32[]{:S(2)}) collective-permute-start(bf16[1024,256]{1,0:T(8,128)(2,1)S(1)} %copy-done.64), channel_id=1, source_target_pairs={{0,16},{4,20},{8,24},{12,28},{16,0},{20,4},{24,8},{28,12},{1,17},{... | collective-permute-start | bytes 1572872 | tf_op jit(solution)/shard_map/ppermute | solution.py:38
  364.4 23.8 %collective-permute-start.88 = (bf16[512,512]{1,0:T(8,128)(2,1)}, bf16[512,512]{1,0:T(8,128)(2,1)S(1)}, u32[]{:S(2)}, u32[]{:S(2)}) collective-permute-start(bf16[512,512]{1,0:T(8,128)(2,1)} %get-tuple-element.316), channel_id=1, source_target_pairs={{1,2},{2,1},{5,6},{6,5},{9,10},{10,9},{13,14},{14,13},{17,18},{18,... | collective-permute-start | bytes 1572872 | tf_op jit(solution)/shard_map/ppermute | solution.py:105
  378.1 25.4 %collective-permute-start.87 = (bf16[512,512]{1,0:T(8,128)(2,1)S(1)}, bf16[512,512]{1,0:T(8,128)(2,1)S(1)}, u32[]{:S(2)}, u32[]{:S(2)}) collective-permute-start(bf16[512,512]{1,0:T(8,128)(2,1)S(1)} %add_convert_fusion.5), channel_id=1, source_target_pairs={{0,2},{1,3},{2,0},{3,1},{4,6},{5,7},{6,4},{7,5},{8,10},{9,11},{10,... | collective-permute-start | bytes 1572872 | tf_op jit(solution)/shard_map/ppermute | solution.py:38
  (85 other events, 1418.3 us)
where the time goes:
time: 437 us; the launch traced here: 431 us
  waiting for transfers between devices  257 us (59%)
  starting transfers between devices  91.5 us (21%)
  Pallas kernels  59.4 us (14%)
  local copies, waits for them, and re-layouts  12.2 us (3%)
  other arithmetic  6.9 us (2%)
    ppermute x65, waiting for transfers between devices, swap(): return lax.ppermute(block, axis, [(i, i ^ step) for i in range(size)])  230 us
    ppermute x65, starting transfers between devices, swap(): return lax.ppermute(block, axis, [(i, i ^ step) for i in range(size)])  77.7 us
    ppermute x2, waiting for transfers between devices, gather_cols(): ends = lax.ppermute(far, 'col', [(2, 3), (1, 0)])  17.3 us
    pallas_call x1, Pallas kernels, retain(): pl.pallas_call(functools.partial(retain_kernel, rows, counts, heads), out...  15.1 us
    pallas_call x1, Pallas kernels, feed(): pl.pallas_call(functools.partial(feed_kernel, rows, counts, tile), out_sh...  11.6 us
    ppermute x2, waiting for transfers between devices, collect(): ends = lax.ppermute(terms[3], 'col', [(3, 2), (0, 1)])  9.5 us
  transfers between devices with their start and end apart: 73, of which 36 were waited for; matrix products, arithmetic and copies ran while one was open for 2% of the time, Pallas kernels for 11%

commit v1 on v0

--- a/solution.py
+++ b/solution.py
@@ -42,33 +42,33 @@
     return lax.optimization_barrier((value,) + earlier)[0]
 
 
-def gather_rows(block, direct=False, behind=()):
+def gather_rows(block, direct=False, halves=(), whole=(), core=()):
     size = lax.axis_size("row")
     pieces = {0: block}
     if size == 8:
-        half = block.shape[0] // 2
+        axis = block.ndim - 2
+        half = block.shape[axis] // 2
         pieces[2] = swap(block, "row", 2)
         pieces[4] = swap(block, "row", 4)
         if direct:
             pieces[6] = swap(block, "row", 6)
         else:
-            across, along = pieces[2], pieces[4]
-            if behind:
-                across, along = after((across, along), *behind)
-            upper = swap(along[:half], "row", 2)
-            lower = swap(across[half:], "row", 4)
-            pieces[6] = jnp.concatenate([upper, lower], axis=0)
+            across, along = after((pieces[2], pieces[4]), *halves)
+            upper = swap(lax.slice_in_dim(along, 0, half, axis=axis), "row", 2)
+            lower = swap(lax.slice_in_dim(across, half, 2 * half, axis=axis), "row", 4)
+            pieces[6] = jnp.concatenate(after((upper, lower), *whole), axis=axis)
+        pieces[0] = after(block, pieces[2], pieces[4])
         bits = [1]
     else:
         bits = [1 << i for i in reversed(range(size.bit_length() - 1))]
     for bit in bits:
         for j in sorted(pieces):
-            pieces[j | bit] = swap(pieces[j], "row", bit)
+            pieces[j | bit] = swap(after(pieces[j], *core), "row", bit)
     return [pieces[j] for j in range(size)]
 
 
 def last_parts(pieces):
-    return (pieces[6], pieces[1], pieces[3], pieces[5]) if len(pieces) == 8 else (pieces[-1],)
+    return (pieces[6],) if len(pieces) == 8 else (pieces[-1],)
 
 
 def gather_lengths(lengths):
@@ -90,43 +90,51 @@
         return [(block,)] + [(swap(block, "col", k),) for k in range(1, size)]
     near = swap(block, "col", 1)
     far = swap(block, "col", 2)
-    middle = lax.ppermute(block, "col", [(1, 2), (2, 1)])
+    middle = lax.ppermute(after(block, far), "col", [(1, 2), (2, 1)])
     ends = lax.ppermute(far, "col", [(2, 3), (1, 0)])
     return [(block,), (near,), (far,), (middle, ends)]
 
 
 def collect(terms):
-    size = lax.axis_size("col")
-    if size != 4:
-        parts = exchange(terms)
-    else:
-        ends = lax.ppermute(terms[3], "col", [(3, 2), (0, 1)])
-        near = swap(terms[1], "col", 1)
-        middle = lax.ppermute(terms[3], "col", [(1, 2), (2, 1)])
-        both = terms[2].astype(jnp.float32) + ends.astype(jnp.float32)
-        far = swap(both.astype(jnp.bfloat16), "col", 2)
-        parts = [terms[0], near, far, middle]
+    if lax.axis_size("col") != 4:
+        return exchange(terms)
+    early = lax.ppermute(terms[3], "col", [(3, 2), (0, 1)])
+    middle = lax.ppermute(terms[3], "col", [(1, 2), (2, 1)])
+    near = swap(after(terms[1], early), "col", 1)
+    both = terms[2].astype(jnp.float32) + early.astype(jnp.float32)
+    far = swap(both.astype(jnp.bfloat16), "col", 2)
+    return [terms[0], near, far, middle]
+
+
+def added(parts):
     return sum(part.astype(jnp.float32) for part in parts)
 
 
-def cut_kernel(cols, place, *refs):
-    masters, outs = refs[:-cols], refs[-cols:]
-    width = outs[0].shape[-1]
+def cut_front_kernel(cols, place, qkvg, out, *blocks):
+    units = out.shape[1] // cols
+    width = blocks[0].shape[1] - units
     for k in range(cols):
         target = lax.bitwise_xor(place[1], k)
         columns = pl.ds(pl.multiple_of(target * width, 128), width)
-        if len(masters) == 1:
-            outs[k][...] = masters[0][:, columns].astype(jnp.bfloat16)
-        else:
-            outs[k][0] = masters[0][:, columns].astype(jnp.bfloat16)
-            outs[k][1] = masters[1][0, :, columns].astype(jnp.bfloat16)
-            outs[k][2] = masters[1][1, :, columns].astype(jnp.bfloat16)
-
-
-def cut(shape, place, *masters):
+        blocks[k][:, :width] = qkvg[:, columns].astype(jnp.bfloat16)
+        columns = pl.ds(pl.multiple_of(target * units, 128), units)
+        blocks[k][:, width:] = out[:, columns].astype(jnp.bfloat16)
+
+
+def cut_feed_kernel(cols, place, down, gateup, *blocks):
+    units = blocks[0].shape[2]
+    for k in range(cols):
+        target = lax.bitwise_xor(place[1], k)
+        columns = pl.ds(pl.multiple_of(target * units, 128), units)
+        blocks[k][0] = down[:, columns].astype(jnp.bfloat16)
+        blocks[k][1] = gateup[0, :, columns].astype(jnp.bfloat16)
+        blocks[k][2] = gateup[1, :, columns].astype(jnp.bfloat16)
+
+
+def cut(kernel, shape, place, *masters):
     cols = lax.axis_size("col")
     return pl.pallas_call(
-        functools.partial(cut_kernel, cols),
+        functools.partial(kernel, cols),
         out_shape=[jax.ShapeDtypeStruct(shape, jnp.bfloat16)] * cols,
         in_specs=[SMEM] + [VMEM] * len(masters),
         out_specs=[VMEM] * cols,
@@ -135,41 +143,29 @@
     )(place, *masters)
 
 
-def turned(values):
-    return values.astype(jnp.float32).T.astype(jnp.bfloat16)
-
-
-def join_kernel(cols, kind, place, *refs):
+def join_kernel(cols, place, *refs):
+    out = refs[cols]
     rows = refs[0].shape[-2]
     for k in range(cols):
         source = lax.bitwise_xor(place[1], k)
         where = pl.ds(pl.multiple_of(source * rows, 16), rows)
-        if kind == "qkvg":
-            refs[cols][where, :] = refs[k][...]
-        elif kind == "out":
-            refs[cols + 1][where, :] = refs[k][...]
+        if len(out.shape) == 2:
+            out[where, :] = refs[k][...]
         else:
-            refs[cols + 2][where, :] = refs[k][0]
-            refs[cols][0, where, :] = refs[k][1]
-            refs[cols][1, where, :] = refs[k][2]
-    if kind == "out":
-        refs[cols][...] = turned(refs[cols + 1][...])
-    elif kind == "feed":
-        refs[cols + 1][...] = turned(refs[cols + 2][...])
-
-
-def join(kind, blocks, place):
+            out[:, where, :] = refs[k][...]
+
+
+def join(blocks, place):
     cols = len(blocks)
-    depth, width = blocks[0].shape[-2] * cols, blocks[0].shape[-1]
-    shapes = {"qkvg": [(depth, width)], "out": [(width, depth)], "feed": [(2, depth, width), (width, depth)]}[kind]
-    return pl.pallas_call(
-        functools.partial(join_kernel, cols, kind),
-        out_shape=[jax.ShapeDtypeStruct(shape, jnp.bfloat16) for shape in shapes],
+    shape = list(blocks[0].shape)
+    shape[-2] *= cols
+    return pl.pallas_call(
+        functools.partial(join_kernel, cols),
+        out_shape=jax.ShapeDtypeStruct(tuple(shape), jnp.bfloat16),
         in_specs=[SMEM] + [VMEM] * cols,
-        out_specs=[VMEM] * len(shapes),
-        scratch_shapes=[] if kind == "qkvg" else [pltpu.VMEM((depth, width), jnp.bfloat16)],
-        compiler_params=params(),
-        cost_estimate=cost(0, 4 * math.prod(blocks[0].shape) * cols),
+        out_specs=VMEM,
+        compiler_params=params(),
+        cost_estimate=cost(0, 4 * math.prod(shape)),
     )(place, *blocks)
 
 
@@ -317,6 +313,10 @@
 DOT = functools.partial(jnp.dot, preferred_element_type=jnp.float32)
 
 
+def DOT_T(left, right):
+    return lax.dot_general(left, right, (((1,), (1,)), ((), ())), preferred_element_type=jnp.float32)
+
+
 def flatten(parts):
     return [part for entry in parts for part in entry], tuple(len(entry) for entry in parts)
 
@@ -381,7 +381,7 @@
         both = project(head, 0)
         query = rotate(both[:, :KEY]).astype(jnp.bfloat16)
         keyed = (rotate(both[:, KEY:]) * (1.0 / math.sqrt(KEY))).astype(jnp.bfloat16)
-        scores = lax.dot_general(query, keyed, (((1,), (1,)), ((), ())), preferred_element_type=jnp.float32)
+        scores = DOT_T(query, keyed)
         scores = scores * jnp.exp(span * decays[head])
         denom = jnp.sum(scores, axis=1, keepdims=True)
         value = project(head, 1)
@@ -412,13 +412,13 @@
     )(place, decays, cosine, sine, seg_col, seg_row, *flat, *weights)
 
 
-def load_terms(rows, cols, place, weights, gathered, sem):
+def load_terms(rows, cols, place, views, gathered, sem):
     ratio = rows // cols
     for j in range(rows):
         owner = lax.bitwise_xor(place[0], j)
         target = owner // ratio
         slot = lax.bitwise_xor(target, place[1]) * ratio + (owner - target * ratio)
-        pltpu.make_async_copy(weights[j], gathered.at[slot], sem).start()
+        pltpu.make_async_copy(views[j], gathered.at[slot], sem).start()
 
 
 def put_terms(rows, cols, left, gathered, sem, outs):
@@ -427,13 +427,15 @@
     pltpu.make_async_copy(gathered, gathered, sem).wait()
     for slot in range(rows):
         k, i = slot // ratio, slot % ratio
-        outs[k][:, i * depth : (i + 1) * depth] = DOT(left, gathered[slot]).astype(jnp.bfloat16)
+        outs[k][:, i * depth : (i + 1) * depth] = DOT_T(left, gathered[slot]).astype(jnp.bfloat16)
 
 
 def mix_kernel(rows, cols, place, mixed, *refs):
     weights, outs = refs[:rows], refs[rows : rows + cols]
     gathered, sem = refs[rows + cols :]
-    load_terms(rows, cols, place, weights, gathered, sem)
+    units = mixed.shape[1]
+    views = [ref.at[:, pl.ds(ref.shape[1] - units, units)] for ref in weights]
+    load_terms(rows, cols, place, views, gathered, sem)
     put_terms(rows, cols, mixed[...], gathered, sem, outs)
 
 
@@ -446,7 +448,7 @@
         in_specs=[SMEM, VMEM] + [ANY] * rows,
         out_specs=[VMEM] * cols,
         scratch_shapes=[
-            pltpu.VMEM((rows,) + weights[0].shape, jnp.bfloat16),
+            pltpu.VMEM((rows, D // rows, mixed.shape[1]), jnp.bfloat16),
             pltpu.SemaphoreType.DMA,
         ],
         compiler_params=params(),
@@ -457,10 +459,9 @@
 def feed_kernel(rows, counts, tile, place, *refs):
     cols, number = len(counts), sum(counts)
     tokens = refs[:number]
-    pairs = refs[number : number + rows]
-    downs = refs[number + rows : number + 2 * rows]
-    outs = refs[number + 2 * rows : number + 2 * rows + cols]
-    ordered, hidden, gathered, gathered_down, sems, sem_down = refs[number + 2 * rows + cols :]
+    weights = refs[number : number + rows]
+    outs = refs[number + rows : number + rows + cols]
+    ordered, hidden, gathered, gathered_down, sems, sem_down = refs[number + rows + cols :]
     depth = D // rows
     width = D // cols
     steps = gathered.shape[2] // tile
@@ -470,9 +471,9 @@
         for j in range(rows):
             where = pl.ds(pl.multiple_of(lax.bitwise_xor(place[0], j) * depth, depth), depth)
             pltpu.make_async_copy(
-                pairs[j].at[:, :, columns], gathered.at[:, where, columns], sems.at[step]
+                weights[j].at[pl.ds(1, 2), :, columns], gathered.at[:, where, columns], sems.at[step]
             ).start()
-    load_terms(rows, cols, place, downs, gathered_down, sem_down)
+    load_terms(rows, cols, place, [ref.at[0] for ref in weights], gathered_down, sem_down)
 
     total = jnp.zeros((S, 1), jnp.float32)
     for k, block in enumerate(read_parts(tokens, counts)):
@@ -492,27 +493,27 @@
     put_terms(rows, cols, hidden[...], gathered_down, sem_down, outs)
 
 
-def feed(place, tokens, gateups, downs):
-    rows, cols = len(gateups), len(tokens)
-    units = gateups[0].shape[2]
+def feed(place, tokens, weights):
+    rows, cols = len(weights), len(tokens)
+    units = weights[0].shape[2]
     tile = min(units, 512)
     flat, counts = flatten(tokens)
     return pl.pallas_call(
         functools.partial(feed_kernel, rows, counts, tile),
         out_shape=[jax.ShapeDtypeStruct((S, D // cols), jnp.bfloat16)] * cols,
-        in_specs=[SMEM] + [VMEM] * len(flat) + [ANY] * (2 * rows),
+        in_specs=[SMEM] + [VMEM] * len(flat) + [ANY] * rows,
         out_specs=[VMEM] * cols,
         scratch_shapes=[
             pltpu.VMEM((S, D), jnp.bfloat16),
             pltpu.VMEM((S, units), jnp.bfloat16),
             pltpu.VMEM((2, D, units), jnp.bfloat16),
-            pltpu.VMEM((rows,) + downs[0].shape, jnp.bfloat16),
+            pltpu.VMEM((rows, D // rows, units), jnp.bfloat16),
             pltpu.SemaphoreType.DMA((units // tile,)),
             pltpu.SemaphoreType.DMA,
         ],
         compiler_params=params(),
         cost_estimate=cost(6 * S * D * units, 6 * D * units),
-    )(place, *flat, *gateups, *downs)
+    )(place, *flat, *weights)
 
 
 def shards(hidden_states, lengths, qkvg_master, gateup_master, out_master, down_master):
@@ -524,12 +525,11 @@
     all_lengths = gather_lengths(lengths)
     depth = qkvg_master.shape[0]
     units = gateup_master.shape[2] // cols
-    qkvg_parts = exchange(cut((depth, heads * HEAD_WIDTH), place, qkvg_master))
-    everyone = gather_rows(after(hidden_states, all_lengths), behind=(qkvg_parts[1],))
-    (qkvg_blocks,) = join("qkvg", qkvg_parts, place)
-    out_cut = cut((depth, units), place, out_master.T)
-    out_parts = exchange(list(after(tuple(out_cut), *qkvg_parts[1:])))
-    (out_blocks,) = join("out", out_parts, place)
+    width = heads * HEAD_WIDTH
+    front_cut = cut(cut_front_kernel, (depth, width + units), place, qkvg_master, out_master.T)
+    front_parts = exchange(front_cut)
+    everyone = gather_rows(after(hidden_states, all_lengths), halves=front_parts[1:3])
+    front_blocks = join(front_parts, place)
 
     table, bins, starts, count = pack(place, all_lengths, rows)
 
@@ -546,28 +546,27 @@
         own = pick(place, table, everyone, turn)
         return own, (jnp.cos(angle), jnp.sin(angle), seg[:, None], seg[None, :])
 
-    table = after(table, *out_parts[1:])
     own, tables = begin(0)
     tokens = gather_cols(own)
-    qkvg_pieces = gather_rows(after(qkvg_blocks, *last_parts(everyone)), behind=[entry[0] for entry in tokens[1:]] + out_parts[1:])
-    out_pieces = gather_rows(after(out_blocks, *last_parts(qkvg_pieces)), direct=True)
-
-    feed_cut = cut((3, depth, units), place, down_master.T, gateup_master)
-    behind = [part for entry in tokens[1:] for part in entry] + qkvg_pieces[1:]
-    feed_parts = exchange(list(after(tuple(feed_cut), *behind)))
-
-    mixed = retain(place, decays, *tables, tokens, qkvg_pieces)
-
-    gateup_blocks, down_blocks = join("feed", list(after(tuple(feed_parts), mixed)), place)
-    gateup_pieces = gather_rows(gateup_blocks)
-    down_pieces = gather_rows(after(down_blocks, *last_parts(gateup_pieces)), direct=True)
-
-    def layer(own, mixed):
-        residual = own.astype(jnp.float32) + collect(mix(place, mixed, out_pieces, cols))
-        terms = feed(place, gather_cols(residual.astype(jnp.bfloat16)), gateup_pieces, down_pieces)
-        return gather_rows((residual + collect(terms)).astype(jnp.bfloat16), direct=True)
-
-    first = layer(own, mixed)
+    ahead = [tokens[1][0], tokens[2][0]]
+    rest = [part for entry in tokens[3:] for part in entry]
+    front_pieces = gather_rows(after(front_blocks, *last_parts(everyone)), halves=ahead, whole=rest)
+
+    feed_cut = cut(cut_feed_kernel, (3, depth, units), place, down_master.T, gateup_master)
+    feed_parts = exchange(list(after(tuple(feed_cut), *rest)))
+
+    mixed = retain(place, decays, *tables, tokens, front_pieces)
+    terms = mix(place, mixed, front_pieces, cols)
+    attended = collect(terms)
+    feed_blocks = join(list(after(tuple(feed_parts), terms[0])), place)
+    feed_pieces = gather_rows(feed_blocks, halves=attended[1:])
+    residual = own.astype(jnp.float32) + added(attended)
+
+    def rest_of_layer(residual):
+        terms = feed(place, gather_cols(residual.astype(jnp.bfloat16)), feed_pieces)
+        return gather_rows((residual + added(collect(terms))).astype(jnp.bfloat16), direct=True)
+
+    first = rest_of_layer(residual)
 
     def finish(pieces):
         return spread(place, lengths, bins, starts, pieces, rows, per_row)
@@ -575,11 +574,13 @@
     def more(pieces):
         for turn in range(1, per_row):
             own, tables = begin(turn)
-            pieces = pieces + layer(own, retain(place, decays, *tables, gather_cols(own), qkvg_pieces))
+            mixed = retain(place, decays, *tables, gather_cols(own), front_pieces)
+            attended = collect(mix(place, mixed, front_pieces, cols))
+            pieces = pieces + rest_of_layer(own.astype(jnp.float32) + added(attended))
         return finish(pieces)
 
     layer_output = lax.cond(count[0] > rows, more, finish, first)
-    return (layer_output, qkvg_blocks, gateup_blocks, out_blocks, down_blocks)
+    return (layer_output, front_blocks[:, :width], feed_blocks[1:], front_blocks[:, width:].T, feed_blocks[0].T)
 
 
 def solution(mesh):

time: 437 us -> 373 us (0.85)
  waiting for transfers between devices: 257 us -> 215 us
  starting transfers between devices: 91.5 us -> 62.9 us
  local copies, waits for them, and re-layouts: 12.2 us -> 26.6 us
  Pallas kernels: 59.4 us -> 53.1 us
    ppermute x65 -> x48, waiting for transfers between devices: 230 us -> 162 us  [swap(): return lax.ppermute(block, axis, [(i, i ^ step) for i in range(size)])]
    ppermute x65 -> x48, starting transfers between devices: 77.7 us -> 45.3 us  [swap(): return lax.ppermute(block, axis, [(i, i ^ step) for i in range(size)])]
    ppermute x2, waiting for transfers between devices: 17.3 us -> 33.6 us  [gather_cols(): ends = lax.ppermute(far, 'col', [(2, 3), (1, 0)])]
    ppermute x4, waiting for transfers between devices: 9.51 us -> 18.8 us  [the longest x2 18.8 us: collect(): early = lax.ppermute(terms[3], 'col', [(3, 2), (0, 1)])]
    unnamed x91 -> x73, local copies, waits for them, and re-layouts: 5.14 us -> 12.8 us
    pallas_call x6 -> x4, Pallas kernels: 16.1 us -> 10.1 us  [the longest x2 6.92 us: cut(): pl.pallas_call(functools.partial(kernel, cols), out_shape=[jax.ShapeDtype...]
  transfers between devices with their start and end apart: 73 -> 56, of which waited for: 36 -> 28; matrix products, arithmetic and copies ran while one was open for 2% -> 6% of each run, Pallas kernels for 11% -> 10%
where the time goes in v1:
time: 373 us; the launch traced here: 370 us
  waiting for transfers between devices  215 us (58%)
  starting transfers between devices  62.9 us (17%)
  Pallas kernels  53.1 us (14%)
  local copies, waits for them, and re-layouts  26.6 us (7%)
  other arithmetic  8.88 us (2%)
    ppermute x48, waiting for transfers between devices, swap(): return lax.ppermute(block, axis, [(i, i ^ step) for i in range(size)])  162 us
    ppermute x48, starting transfers between devices, swap(): return lax.ppermute(block, axis, [(i, i ^ step) for i in range(size)])  45.3 us
    ppermute x2, waiting for transfers between devices, gather_cols(): ends = lax.ppermute(far, 'col', [(2, 3), (1, 0)])  33.6 us
    ppermute x2, waiting for transfers between devices, collect(): early = lax.ppermute(terms[3], 'col', [(3, 2), (0, 1)])  18.8 us
    pallas_call x1, Pallas kernels, retain(): pl.pallas_call(functools.partial(retain_kernel, rows, counts, heads), out...  14.2 us
    unnamed x73, local copies, waits for them, and re-layouts  12.8 us
    ppermute x2, starting transfers between devices, collect(): early = lax.ppermute(terms[3], 'col', [(3, 2), (0, 1)])  11.9 us
    pallas_call x1, Pallas kernels, feed(): pl.pallas_call(functools.partial(feed_kernel, rows, counts, tile), out_sh...  11.8 us
  transfers between devices with their start and end apart: 56, of which 28 were waited for; matrix products, arithmetic and copies ran while one was open for 6% of the time, Pallas kernels for 10%

profile of v1, /device:TPU:0, one launch (start us, length us, event | category | flops | bytes accessed | tf_op | source)
XLA Modules:
  0.0 369.7 jit_solution(550951722024212287)
XLA Ops:
  2.8 2.8 collective-permute-start.24
  16.4 3.7 %shard_map.102 = (bf16[64,4096]{1,0:T(8,128)(2,1)}, bf16[64,4096]{1,0:T(8,128)(2,1)}, bf16[64,4096]{1,0:T(8,128)(2,1)}, bf16[64,4096]{1,0:T(8,128)(2,1)}) custom-call(s32[2]{0:T(128)S(1)} %pad_add_fusion.place, f32[64,12288]{1,0:T(8,128)} %qkvg.1, f32[64,4096]{1,0:T(8,128)} %bitcast.11), custom_call_target="tpu_custom_call" | custom-call | bytes 6291456 | tf_op jit(solution)/shard_map/pallas_call | solution.py:136
  24.4 16.2 %collective-permute-done.31.refs_1_ = bf16[64,4096]{1,0:T(8,128)(2,1)S(1)} collective-permute-done((bf16[64,4096]{1,0:T(8,128)(2,1)}, bf16[64,4096]{1,0:T(8,128)(2,1)S(1)}, u32[]{:S(2)}, u32[]{:S(2)}) %collective-permute-start.31) | collective-permute-done | bytes 524320 | tf_op jit(solution)/shard_map/ppermute | solution.py:38
  40.7 19.4 %collective-permute-done.32.refs_2_ = bf16[64,4096]{1,0:T(8,128)(2,1)S(1)} collective-permute-done((bf16[64,4096]{1,0:T(8,128)(2,1)}, bf16[64,4096]{1,0:T(8,128)(2,1)S(1)}, u32[]{:S(2)}, u32[]{:S(2)}) %collective-permute-start.32) | collective-permute-done | bytes 524320 | tf_op jit(solution)/shard_map/ppermute | solution.py:38
  64.6 4.8 %collective-permute-done.33 = bf16[512,512]{1,0:T(8,128)(2,1)S(1)} collective-permute-done((bf16[512,512]{1,0:T(8,128)(2,1)S(1)}, bf16[512,512]{1,0:T(8,128)(2,1)S(1)}, u32[]{:S(2)}, u32[]{:S(2)}) %collective-permute-start.33) | collective-permute-done | bytes 524320 | tf_op jit(solution)/shard_map/ppermute | solution.py:38
  75.9 4.1 %shard_map.101 = (s32[64]{0:T(128)S(1)}, s32[16]{0:T(128)S(1)}, s32[16]{0:T(128)S(1)}, s32[1]{0:T(128)}) custom-call(s32[2]{0:T(128)S(1)} %pad_add_fusion.place, s32[16]{0:T(128)} %pad_add_fusion.3.lengths), custom_call_target="tpu_custom_call" | custom-call | tf_op jit(solution)/shard_map/pallas_call | solution.py:221
  81.1 3.8 %shard_map.103.refs_0_ = bf16[512,512]{1,0:T(8,128)(2,1)} custom-call(s32[2]{0:T(128)S(1)} %pad_add_fusion.place, s32[64]{0:T(128)S(1)} %get-tuple-element.233.table, bf16[1024,512]{1,0:T(8,128)(2,1)S(1)} %copy-done.8, bf16[1024,512]{1,0:T(8,128)(2,1)S(1)} %collective-permute-done.28.refs_1_, bf16[1024,512]{1,0:T(8,128)(2,1)S(1)} %collective-permute-done.26.refs_2_, ...), custom_call_target="tpu_custom_call" | custom-call | bytes 1048576 | tf_op jit(solution)/shard_map/pallas_call | solution.py:258
  85.0 3.0 collective-permute-start.37
  88.1 21.8 %collective-permute-done.36.refs_1_ = bf16[512,512]{1,0:T(8,128)(2,1)S(1)} collective-permute-done((bf16[512,512]{1,0:T(8,128)(2,1)}, bf16[512,512]{1,0:T(8,128)(2,1)S(1)}, u32[]{:S(2)}, u32[]{:S(2)}) %collective-permute-start.36) | collective-permute-done | bytes 524320 | tf_op jit(solution)/shard_map/ppermute | solution.py:38
  111.3 5.5 %collective-permute-done.41.refs_7_.refs_2_ = bf16[256,4096]{1,0:T(8,128)(2,1)} collective-permute-done((bf16[256,4096]{1,0:T(8,128)(2,1)S(1)}, bf16[256,4096]{1,0:T(8,128)(2,1)}, u32[]{:S(2)}, u32[]{:S(2)}) %collective-permute-start.41) | collective-permute-done | bytes 2097184 | tf_op jit(solution)/shard_map/ppermute | solution.py:38
  125.2 9.1 %collective-permute-done.39.refs_4_ = bf16[512,512]{1,0:T(8,128)(2,1)S(1)} collective-permute-done((bf16[512,512]{1,0:T(8,128)(2,1)S(1)}, bf16[512,512]{1,0:T(8,128)(2,1)S(1)}, u32[]{:S(2)}, u32[]{:S(2)}) %collective-permute-start.39) | collective-permute-done | bytes 524320 | tf_op jit(solution)/shard_map/ppermute | solution.py:94
  134.3 3.8 %collective-permute-done.46 = bf16[128,4096]{1,0:T(8,128)(2,1)S(1)} collective-permute-done((bf16[128,4096]{1,0:T(8,128)(2,1)S(1)}, bf16[128,4096]{1,0:T(8,128)(2,1)S(1)}, u32[]{:S(2)}, u32[]{:S(2)}) %collective-permute-start.46) | collective-permute-done | bytes 1048608 | tf_op jit(solution)/shard_map/ppermute | solution.py:38
  141.6 3.2 shard_map.107
  153.3 14.2 %shard_map.105.mixed = bf16[512,1024]{1,0:T(8,128)(2,1)} custom-call(s32[2]{0:T(128)S(1)} %pad_add_fusion.place, f32[2]{0:T(128)S(1)} %negate_log-plus-one_fusion.decays, f32[512,128]{1,0:T(8,128)} %get-tuple-element.295.cosine, f32[512,128]{1,0:T(8,128)} %get-tuple-element.294.sine, s32[512,1]{1,0:T(8,128)} %broadcast_in_dim_reshape.8.seg_col, ...), custom_call_target="tpu_custom_call" | custom-call | flops 8375186432 | bytes 12582912 | tf_op jit(solution)/shard_map/pallas_call | solution.py:400
  167.5 6.5 %shard_map.106 = (bf16[512,512]{1,0:T(8,128)(2,1)}, bf16[512,512]{1,0:T(8,128)(2,1)}, bf16[512,512]{1,0:T(8,128)(2,1)}, bf16[512,512]{1,0:T(8,128)(2,1)}) custom-call(s32[2]{0:T(128)S(1)} %pad_add_fusion.place, bf16[512,1024]{1,0:T(8,128)(2,1)} %shard_map.105.mixed, bf16[256,4096]{1,0:T(8,128)(2,1)S(1)} %shard_map.104.refs_5_.refs_0_, ...), custom_call_target="tpu_custom_call" | custom-call | flops 2147483648 | bytes 4194304 | tf_op jit(solution)/shard_map/pallas_call | solution.py:445
  174.1 6.4 %collective-permute-done.58.refs_2_ = bf16[3,64,1024]{2,1,0:T(8,128)(2,1)S(1)} collective-permute-done((bf16[3,64,1024]{2,1,0:T(8,128)(2,1)}, bf16[3,64,1024]{2,1,0:T(8,128)(2,1)S(1)}, u32[]{:S(2)}, u32[]{:S(2)}) %collective-permute-start.58) | collective-permute-done | bytes 393248 | tf_op jit(solution)/shard_map/ppermute | solution.py:38
  184.2 10.4 %collective-permute-start.49 = (bf16[512,512]{1,0:T(8,128)(2,1)}, bf16[512,512]{1,0:T(8,128)(2,1)S(1)}, u32[]{:S(2)}, u32[]{:S(2)}) collective-permute-start(bf16[512,512]{1,0:T(8,128)(2,1)} %get-tuple-element.253), channel_id=1, source_target_pairs={{3,2},{0,1},{7,6},{4,5},{11,10},{8,9},{15,14},{12,13},{19,18},{16,... | collective-permute-start | bytes 1572872 | tf_op jit(solution)/shard_map/ppermute | solution.py:101
  195.5 9.9 %collective-permute-done.49 = bf16[512,512]{1,0:T(8,128)(2,1)S(1)} collective-permute-done((bf16[512,512]{1,0:T(8,128)(2,1)}, bf16[512,512]{1,0:T(8,128)(2,1)S(1)}, u32[]{:S(2)}, u32[]{:S(2)}) %collective-permute-start.49) | collective-permute-done | bytes 524320 | tf_op jit(solution)/shard_map/ppermute | solution.py:101
  208.8 20.3 %collective-permute-done.50 = bf16[512,512]{1,0:T(8,128)(2,1)S(1)} collective-permute-done((bf16[512,512]{1,0:T(8,128)(2,1)}, bf16[512,512]{1,0:T(8,128)(2,1)S(1)}, u32[]{:S(2)}, u32[]{:S(2)}) %collective-permute-start.50) | collective-permute-done | bytes 524320 | tf_op jit(solution)/shard_map/ppermute | solution.py:38
  229.2 2.7 collective-permute-done.51
  234.8 2.9 collective-permute-start.53
  237.8 8.6 %collective-permute-done.65 = bf16[3,128,1024]{2,1,0:T(8,128)(2,1)S(1)} collective-permute-done((bf16[3,128,1024]{2,1,0:T(8,128)(2,1)S(1)}, bf16[3,128,1024]{2,1,0:T(8,128)(2,1)S(1)}, u32[]{:S(2)}, u32[]{:S(2)}) %collective-permute-start.65) | collective-permute-done | bytes 786464 | tf_op jit(solution)/shard_map/ppermute | solution.py:38
  247.1 8.1 %collective-permute-done.54.refs_2_ = bf16[512,512]{1,0:T(8,128)(2,1)S(1)} collective-permute-done((bf16[512,512]{1,0:T(8,128)(2,1)S(1)}, bf16[512,512]{1,0:T(8,128)(2,1)S(1)}, u32[]{:S(2)}, u32[]{:S(2)}) %collective-permute-start.54) | collective-permute-done | bytes 524320 | tf_op jit(solution)/shard_map/ppermute | solution.py:38
  257.2 24.5 %collective-permute-done.56.refs_4_ = bf16[512,512]{1,0:T(8,128)(2,1)S(1)} collective-permute-done((bf16[512,512]{1,0:T(8,128)(2,1)S(1)}, bf16[512,512]{1,0:T(8,128)(2,1)S(1)}, u32[]{:S(2)}, u32[]{:S(2)}) %collective-permute-start.56) | collective-permute-done | bytes 524320 | tf_op jit(solution)/shard_map/ppermute | solution.py:94
  284.8 11.8 %shard_map.109 = (bf16[512,512]{1,0:T(8,128)(2,1)}, bf16[512,512]{1,0:T(8,128)(2,1)}, bf16[512,512]{1,0:T(8,128)(2,1)}, bf16[512,512]{1,0:T(8,128)(2,1)}) custom-call(s32[2]{0:T(128)S(1)} %pad_add_fusion.place, bf16[512,512]{1,0:T(8,128)(2,1)} %copy-done.26, bf16[512,512]{1,0:T(8,128)(2,1)} %copy-done.44, bf16[512,512]{1,0:T(8,128)(2,1)} %copy-done.43, ...), custom_call_target="tpu_custom_call" | custom-call | flops 6442450944 | bytes 12582912 | tf_op jit(solution)/shard_map/pallas_call | solution.py:501
  298.7 9.0 %collective-permute-done.68 = bf16[512,512]{1,0:T(8,128)(2,1)S(1)} collective-permute-done((bf16[512,512]{1,0:T(8,128)(2,1)}, bf16[512,512]{1,0:T(8,128)(2,1)S(1)}, u32[]{:S(2)}, u32[]{:S(2)}) %collective-permute-start.68) | collective-permute-done | bytes 524320 | tf_op jit(solution)/shard_map/ppermute | solution.py:101
  311.3 14.7 %collective-permute-done.69 = bf16[512,512]{1,0:T(8,128)(2,1)S(1)} collective-permute-done((bf16[512,512]{1,0:T(8,128)(2,1)}, bf16[512,512]{1,0:T(8,128)(2,1)S(1)}, u32[]{:S(2)}, u32[]{:S(2)}) %collective-permute-start.69) | collective-permute-done | bytes 524320 | tf_op jit(solution)/shard_map/ppermute | solution.py:38
  326.0 6.3 %collective-permute-done.70 = bf16[512,512]{1,0:T(8,128)(2,1)S(1)} collective-permute-done((bf16[512,512]{1,0:T(8,128)(2,1)S(1)}, bf16[512,512]{1,0:T(8,128)(2,1)S(1)}, u32[]{:S(2)}, u32[]{:S(2)}) %collective-permute-start.70) | collective-permute-done | bytes 524320 | tf_op jit(solution)/shard_map/ppermute | solution.py:38
  338.3 8.4 %collective-permute-done.72 = bf16[512,512]{1,0:T(8,128)(2,1)} collective-permute-done((bf16[512,512]{1,0:T(8,128)(2,1)}, bf16[512,512]{1,0:T(8,128)(2,1)}, u32[]{:S(2)}, u32[]{:S(2)}) %collective-permute-start.72) | collective-permute-done | bytes 524320 | tf_op jit(solution)/shard_map/ppermute | solution.py:38
  346.7 5.6 %collective-permute-done.73 = bf16[512,512]{1,0:T(8,128)(2,1)} collective-permute-done((bf16[512,512]{1,0:T(8,128)(2,1)}, bf16[512,512]{1,0:T(8,128)(2,1)}, u32[]{:S(2)}, u32[]{:S(2)}) %collective-permute-start.73) | collective-permute-done | bytes 524320 | tf_op jit(solution)/shard_map/ppermute | solution.py:38
  364.4 3.7 %conditional.1 = (bf16[1024,512]{1,0:T(8,128)(2,1)S(1)}) conditional(s32[]{:T(128)} %bitcast.2, (s32[2]{0:T(128)S(1)}, s32[2]{0:T(128)S(1)}, s32[16]{0:T(128)S(1)}, s32[16]{0:T(128)S(1)}, bf16[512,512]{1,0:T(8,128)(2,1)}, /*index=5*/bf16[512,512]{1,0:T(8,128)(2,1)}, bf16[512,512]{1,0:T(8,128)(2,1)}, bf16[512,512]{1,0:T(8,128)(2,1)}, ...), branch_computations={%region_0.1_spmd, %region_1.2_spmd} | conditional | flops 16974625792 | bytes 146298368 | solution.py:582
  364.5 2.6 branch_0_fun.1
  (195 shorter events, 91.7 us)
Async XLA Ops:
  12.8 47.3 %collective-permute-start.26 = (bf16[1024,512]{1,0:T(8,128)(2,1)}, bf16[1024,512]{1,0:T(8,128)(2,1)S(1)}, u32[]{:S(2)}, u32[]{:S(2)}) collective-permute-start(bf16[1024,512]{1,0:T(8,128)(2,1)} %refs_0_), channel_id=1, source_target_pairs={{0,8},{4,12},{8,0},{12,4},{16,24},{20,28},{24,16},{28,20},{1,9},{5... | collective-permute-start | bytes 3145736 | tf_op jit(solution)/shard_map/ppermute | solution.py:38
  14.8 45.3 %collective-permute-start.27 = (bf16[1024,512]{1,0:T(8,128)(2,1)}, bf16[1024,512]{1,0:T(8,128)(2,1)S(1)}, u32[]{:S(2)}, u32[]{:S(2)}) collective-permute-start(bf16[1024,512]{1,0:T(8,128)(2,1)} %refs_0_), channel_id=1, source_target_pairs={{0,16},{4,20},{8,24},{12,28},{16,0},{20,4},{24,8},{28,12},{1,17},{... | collective-permute-start | bytes 3145736 | tf_op jit(solution)/shard_map/ppermute | solution.py:38
  20.1 20.6 %collective-permute-start.31 = (bf16[64,4096]{1,0:T(8,128)(2,1)}, bf16[64,4096]{1,0:T(8,128)(2,1)S(1)}, u32[]{:S(2)}, u32[]{:S(2)}) collective-permute-start(bf16[64,4096]{1,0:T(8,128)(2,1)} %get-tuple-element.236), channel_id=1, source_target_pairs={{0,1},{1,0},{2,3},{3,2},{4,5},{5,4},{6,7},{7,6},{8,9},{9,8},{10,11... | collective-permute-start | bytes 1572872 | tf_op jit(solution)/shard_map/ppermute | solution.py:38
  21.6 38.4 %collective-permute-start.32 = (bf16[64,4096]{1,0:T(8,128)(2,1)}, bf16[64,4096]{1,0:T(8,128)(2,1)S(1)}, u32[]{:S(2)}, u32[]{:S(2)}) collective-permute-start(bf16[64,4096]{1,0:T(8,128)(2,1)} %get-tuple-element.237), channel_id=1, source_target_pairs={{0,2},{1,3},{2,0},{3,1},{4,6},{5,7},{6,4},{7,5},{8,10},{9,11},{10,... | collective-permute-start | bytes 1572872 | tf_op jit(solution)/shard_map/ppermute | solution.py:38
  24.2 37.9 %collective-permute-start.40 = (bf16[64,4096]{1,0:T(8,128)(2,1)}, bf16[64,4096]{1,0:T(8,128)(2,1)S(1)}, u32[]{:S(2)}, u32[]{:S(2)}) collective-permute-start(bf16[64,4096]{1,0:T(8,128)(2,1)} %get-tuple-element.244), channel_id=1, source_target_pairs={{0,3},{1,2},{2,1},{3,0},{4,7},{5,6},{6,5},{7,4},{8,11},{9,10},{10,... | collective-permute-start | bytes 1572872 | tf_op jit(solution)/shard_map/ppermute | solution.py:38
  73.2 43.6 %collective-permute-start.41 = (bf16[256,4096]{1,0:T(8,128)(2,1)S(1)}, bf16[256,4096]{1,0:T(8,128)(2,1)}, u32[]{:S(2)}, u32[]{:S(2)}) collective-permute-start(bf16[256,4096]{1,0:T(8,128)(2,1)S(1)} %shard_map.104.refs_5_.refs_0_), channel_id=1, source_target_pairs={{0,8},{4,12},{8,0},{12,4},{16,24},{20,28},{24,16},{28,20},{1,9},{5... | collective-permute-start | bytes 6291464 | tf_op jit(solution)/shard_map/ppermute | solution.py:38
  74.8 42.2 %collective-permute-start.42 = (bf16[256,4096]{1,0:T(8,128)(2,1)S(1)}, bf16[256,4096]{1,0:T(8,128)(2,1)}, u32[]{:S(2)}, u32[]{:S(2)}) collective-permute-start(bf16[256,4096]{1,0:T(8,128)(2,1)S(1)} %shard_map.104.refs_5_.refs_0_), channel_id=1, source_target_pairs={{0,16},{4,20},{8,24},{12,28},{16,0},{20,4},{24,8},{28,12},{1,17},{... | collective-permute-start | bytes 6291464 | tf_op jit(solution)/shard_map/ppermute | solution.py:38
  85.0 24.9 %collective-permute-start.36 = (bf16[512,512]{1,0:T(8,128)(2,1)}, bf16[512,512]{1,0:T(8,128)(2,1)S(1)}, u32[]{:S(2)}, u32[]{:S(2)}) collective-permute-start(bf16[512,512]{1,0:T(8,128)(2,1)} %shard_map.103.refs_0_), channel_id=1, source_target_pairs={{0,1},{1,0},{2,3},{3,2},{4,5},{5,4},{6,7},{7,6},{8,9},{9,8},{10,11... | collective-permute-start | bytes 1572872 | tf_op jit(solution)/shard_map/ppermute | solution.py:38
  85.0 26.2 %collective-permute-start.37 = (bf16[512,512]{1,0:T(8,128)(2,1)}, bf16[512,512]{1,0:T(8,128)(2,1)S(1)}, u32[]{:S(2)}, u32[]{:S(2)}) collective-permute-start(bf16[512,512]{1,0:T(8,128)(2,1)} %shard_map.103.refs_0_), channel_id=1, source_target_pairs={{0,2},{1,3},{2,0},{3,1},{4,6},{5,7},{6,4},{7,5},{8,10},{9,11},{10,... | collective-permute-start | bytes 1572872 | tf_op jit(solution)/shard_map/ppermute | solution.py:38
  118.3 19.9 %collective-permute-start.46 = (bf16[128,4096]{1,0:T(8,128)(2,1)S(1)}, bf16[128,4096]{1,0:T(8,128)(2,1)S(1)}, u32[]{:S(2)}, u32[]{:S(2)}) collective-permute-start(bf16[128,4096]{1,0:T(8,128)(2,1)S(1)} %slice.39), channel_id=1, source_target_pairs={{0,8},{4,12},{8,0},{12,4},{16,24},{20,28},{24,16},{28,20},{1,9},{5... | collective-permute-start | bytes 3145736 | tf_op jit(solution)/shard_map/ppermute | solution.py:38
  121.9 17.6 %collective-permute-start.47 = (bf16[128,4096]{1,0:T(8,128)(2,1)S(1)}, bf16[128,4096]{1,0:T(8,128)(2,1)S(1)}, u32[]{:S(2)}, u32[]{:S(2)}) collective-permute-start(bf16[128,4096]{1,0:T(8,128)(2,1)S(1)} %slice.40), channel_id=1, source_target_pairs={{0,16},{4,20},{8,24},{12,28},{16,0},{20,4},{24,8},{28,12},{1,17},{... | collective-permute-start | bytes 3145736 | tf_op jit(solution)/shard_map/ppermute | solution.py:38
  124.6 26.0 %collective-permute-start.43 = (bf16[256,4096]{1,0:T(8,128)(2,1)S(1)}, bf16[256,4096]{1,0:T(8,128)(2,1)}, u32[]{:S(2)}, u32[]{:S(2)}) collective-permute-start(bf16[256,4096]{1,0:T(8,128)(2,1)S(1)} %shard_map.104.refs_5_.refs_0_), channel_id=1, source_target_pairs={{0,4},{4,0},{8,12},{12,8},{16,20},{20,16},{24,28},{28,24},{1,5},{5... | collective-permute-start | bytes 6291464 | tf_op jit(solution)/shard_map/ppermute | solution.py:38
  124.7 27.1 %collective-permute-start.44 = (bf16[256,4096]{1,0:T(8,128)(2,1)}, bf16[256,4096]{1,0:T(8,128)(2,1)}, u32[]{:S(2)}, u32[]{:S(2)}) collective-permute-start(bf16[256,4096]{1,0:T(8,128)(2,1)} %collective-permute-done.41.refs_7_.refs_2_), channel_id=1, source_target_pairs={{0,4},{4,0},{8,12},{12,8},{16,20},{20,16},{24,28},{28,24},{1,5},{5... | collective-permute-start | bytes 6291464 | tf_op jit(solution)/shard_map/ppermute | solution.py:38
  134.3 19.0 %collective-permute-start.45 = (bf16[256,4096]{1,0:T(8,128)(2,1)}, bf16[256,4096]{1,0:T(8,128)(2,1)}, u32[]{:S(2)}, u32[]{:S(2)}) collective-permute-start(bf16[256,4096]{1,0:T(8,128)(2,1)} %collective-permute-done.42.refs_9_.refs_4_), channel_id=1, source_target_pairs={{0,4},{4,0},{8,12},{12,8},{16,20},{20,16},{24,28},{28,24},{1,5},{5... | collective-permute-start | bytes 6291464 | tf_op jit(solution)/shard_map/ppermute | solution.py:38
  148.5 25.6 %collective-permute-start.57 = (bf16[3,64,1024]{2,1,0:T(8,128)(2,1)}, bf16[3,64,1024]{2,1,0:T(8,128)(2,1)S(1)}, u32[]{:S(2)}, u32[]{:S(2)}) collective-permute-start(bf16[3,64,1024]{2,1,0:T(8,128)(2,1)} %get-tuple-element.262), channel_id=1, source_target_pairs={{0,1},{1,0},{2,3},{3,2},{4,5},{5,4},{6,7},{7,6},{8,9},{9,8},{10,11... | collective-permute-start | bytes 1179656 | tf_op jit(solution)/shard_map/ppermute | solution.py:38
  150.6 30.0 %collective-permute-start.58 = (bf16[3,64,1024]{2,1,0:T(8,128)(2,1)}, bf16[3,64,1024]{2,1,0:T(8,128)(2,1)S(1)}, u32[]{:S(2)}, u32[]{:S(2)}) collective-permute-start(bf16[3,64,1024]{2,1,0:T(8,128)(2,1)} %get-tuple-element.263), channel_id=1, source_target_pairs={{0,2},{1,3},{2,0},{3,1},{4,6},{5,7},{6,4},{7,5},{8,10},{9,11},{10,... | collective-permute-start | bytes 1179656 | tf_op jit(solution)/shard_map/ppermute | solution.py:38
  151.9 28.7 %collective-permute-start.59 = (bf16[3,64,1024]{2,1,0:T(8,128)(2,1)}, bf16[3,64,1024]{2,1,0:T(8,128)(2,1)S(1)}, u32[]{:S(2)}, u32[]{:S(2)}) collective-permute-start(bf16[3,64,1024]{2,1,0:T(8,128)(2,1)} %get-tuple-element.264), channel_id=1, source_target_pairs={{0,3},{1,2},{2,1},{3,0},{4,7},{5,6},{6,5},{7,4},{8,11},{9,10},{10,... | collective-permute-start | bytes 1179656 | tf_op jit(solution)/shard_map/ppermute | solution.py:38
  182.9 49.0 %collective-permute-start.60 = (bf16[3,256,1024]{2,1,0:T(8,128)(2,1)S(1)}, bf16[3,256,1024]{2,1,0:T(8,128)(2,1)S(1)}, u32[]{:S(2)}, u32[]{:S(2)}) collective-permute-start(bf16[3,256,1024]{2,1,0:T(8,128)(2,1)S(1)} %shard_map.108.refs_5_), channel_id=1, source_target_pairs={{0,8},{4,12},{8,0},{12,4},{16,24},{20,28},{24,16},{28,20},{1,9},{5... | collective-permute-start | bytes 4718600 | tf_op jit(solution)/shard_map/ppermute | solution.py:38
  183.6 48.4 %collective-permute-start.61 = (bf16[3,256,1024]{2,1,0:T(8,128)(2,1)S(1)}, bf16[3,256,1024]{2,1,0:T(8,128)(2,1)S(1)}, u32[]{:S(2)}, u32[]{:S(2)}) collective-permute-start(bf16[3,256,1024]{2,1,0:T(8,128)(2,1)S(1)} %shard_map.108.refs_5_), channel_id=1, source_target_pairs={{0,16},{4,20},{8,24},{12,28},{16,0},{20,4},{24,8},{28,12},{1,17},{... | collective-permute-start | bytes 4718600 | tf_op jit(solution)/shard_map/ppermute | solution.py:38
  184.2 21.2 %collective-permute-start.49 = (bf16[512,512]{1,0:T(8,128)(2,1)}, bf16[512,512]{1,0:T(8,128)(2,1)S(1)}, u32[]{:S(2)}, u32[]{:S(2)}) collective-permute-start(bf16[512,512]{1,0:T(8,128)(2,1)} %get-tuple-element.253), channel_id=1, source_target_pairs={{3,2},{0,1},{7,6},{4,5},{11,10},{8,9},{15,14},{12,13},{19,18},{16,... | collective-permute-start | bytes 1572872 | tf_op jit(solution)/shard_map/ppermute | solution.py:101
  205.3 23.8 %collective-permute-start.50 = (bf16[512,512]{1,0:T(8,128)(2,1)}, bf16[512,512]{1,0:T(8,128)(2,1)S(1)}, u32[]{:S(2)}, u32[]{:S(2)}) collective-permute-start(bf16[512,512]{1,0:T(8,128)(2,1)} %get-tuple-element.254), channel_id=1, source_target_pairs={{0,1},{1,0},{2,3},{3,2},{4,5},{5,4},{6,7},{7,6},{8,9},{9,8},{10,11... | collective-permute-start | bytes 1572872 | tf_op jit(solution)/shard_map/ppermute | solution.py:38
  207.9 24.0 %collective-permute-start.51 = (bf16[512,512]{1,0:T(8,128)(2,1)S(1)}, bf16[512,512]{1,0:T(8,128)(2,1)S(1)}, u32[]{:S(2)}, u32[]{:S(2)}) collective-permute-start(bf16[512,512]{1,0:T(8,128)(2,1)S(1)} %add_convert_fusion.6), channel_id=1, source_target_pairs={{0,2},{1,3},{2,0},{3,1},{4,6},{5,7},{6,4},{7,5},{8,10},{9,11},{10,... | collective-permute-start | bytes 1572872 | tf_op jit(solution)/shard_map/ppermute | solution.py:38
  232.6 22.5 %collective-permute-start.54 = (bf16[512,512]{1,0:T(8,128)(2,1)S(1)}, bf16[512,512]{1,0:T(8,128)(2,1)S(1)}, u32[]{:S(2)}, u32[]{:S(2)}) collective-permute-start(bf16[512,512]{1,0:T(8,128)(2,1)S(1)} %fusion.3.refs_0_), channel_id=1, source_target_pairs={{0,2},{1,3},{2,0},{3,1},{4,6},{5,7},{6,4},{7,5},{8,10},{9,11},{10,... | collective-permute-start | bytes 1572872 | tf_op jit(solution)/shard_map/ppermute | solution.py:38
  234.8 20.3 %collective-permute-start.53 = (bf16[512,512]{1,0:T(8,128)(2,1)S(1)}, bf16[512,512]{1,0:T(8,128)(2,1)S(1)}, u32[]{:S(2)}, u32[]{:S(2)}) collective-permute-start(bf16[512,512]{1,0:T(8,128)(2,1)S(1)} %fusion.3.refs_0_), channel_id=1, source_target_pairs={{0,1},{1,0},{2,3},{3,2},{4,5},{5,4},{6,7},{7,6},{8,9},{9,8},{10,11... | collective-permute-start | bytes 1572872 | tf_op jit(solution)/shard_map/ppermute | solution.py:38
  237.8 43.9 %collective-permute-start.62 = (bf16[3,256,1024]{2,1,0:T(8,128)(2,1)S(1)}, bf16[3,256,1024]{2,1,0:T(8,128)(2,1)S(1)}, u32[]{:S(2)}, u32[]{:S(2)}) collective-permute-start(bf16[3,256,1024]{2,1,0:T(8,128)(2,1)S(1)} %shard_map.108.refs_5_), channel_id=1, source_target_pairs={{0,4},{4,0},{8,12},{12,8},{16,20},{20,16},{24,28},{28,24},{1,5},{5... | collective-permute-start | bytes 4718600 | tf_op jit(solution)/shard_map/ppermute | solution.py:38
  246.4 35.3 %collective-permute-start.63 = (bf16[3,256,1024]{2,1,0:T(8,128)(2,1)S(1)}, bf16[3,256,1024]{2,1,0:T(8,128)(2,1)S(1)}, u32[]{:S(2)}, u32[]{:S(2)}) collective-permute-start(bf16[3,256,1024]{2,1,0:T(8,128)(2,1)S(1)} %collective-permute-done.60.refs_7_), channel_id=1, source_target_pairs={{0,4},{4,0},{8,12},{12,8},{16,20},{20,16},{24,28},{28,24},{1,5},{5... | collective-permute-start | bytes 4718600 | tf_op jit(solution)/shard_map/ppermute | solution.py:38
  246.9 34.8 %collective-permute-start.64 = (bf16[3,256,1024]{2,1,0:T(8,128)(2,1)S(1)}, bf16[3,256,1024]{2,1,0:T(8,128)(2,1)S(1)}, u32[]{:S(2)}, u32[]{:S(2)}) collective-permute-start(bf16[3,256,1024]{2,1,0:T(8,128)(2,1)S(1)} %collective-permute-done.61.refs_9_), channel_id=1, source_target_pairs={{0,4},{4,0},{8,12},{12,8},{16,20},{20,16},{24,28},{28,24},{1,5},{5... | collective-permute-start | bytes 4718600 | tf_op jit(solution)/shard_map/ppermute | solution.py:38
  255.1 29.6 %collective-permute-start.67 = (bf16[3,256,1024]{2,1,0:T(8,128)(2,1)S(1)}, bf16[3,256,1024]{2,1,0:T(8,128)(2,1)}, u32[]{:S(2)}, u32[]{:S(2)}) collective-permute-start(bf16[3,256,1024]{2,1,0:T(8,128)(2,1)S(1)} %constant_dynamic-update-slice_fusion.4.refs_11_), channel_id=1, source_target_pairs={{0,4},{4,0},{8,12},{12,8},{16,20},{20,16},{24,28},{28,24},{1,5},{5... | collective-permute-start | bytes 4718600 | tf_op jit(solution)/shard_map/ppermute | solution.py:38
  255.9 25.8 %collective-permute-start.56 = (bf16[512,512]{1,0:T(8,128)(2,1)S(1)}, bf16[512,512]{1,0:T(8,128)(2,1)S(1)}, u32[]{:S(2)}, u32[]{:S(2)}) collective-permute-start(bf16[512,512]{1,0:T(8,128)(2,1)S(1)} %collective-permute-done.54.refs_2_), channel_id=1, source_target_pairs={{2,3},{1,0},{6,7},{5,4},{10,11},{9,8},{14,15},{13,12},{18,19},{17,... | collective-permute-start | bytes 1572872 | tf_op jit(solution)/shard_map/ppermute | solution.py:94
  307.7 18.3 %collective-permute-start.69 = (bf16[512,512]{1,0:T(8,128)(2,1)}, bf16[512,512]{1,0:T(8,128)(2,1)S(1)}, u32[]{:S(2)}, u32[]{:S(2)}) collective-permute-start(bf16[512,512]{1,0:T(8,128)(2,1)} %get-tuple-element.277), channel_id=1, source_target_pairs={{0,1},{1,0},{2,3},{3,2},{4,5},{5,4},{6,7},{7,6},{8,9},{9,8},{10,11... | collective-permute-start | bytes 1572872 | tf_op jit(solution)/shard_map/ppermute | solution.py:38
  311.2 21.1 %collective-permute-start.70 = (bf16[512,512]{1,0:T(8,128)(2,1)S(1)}, bf16[512,512]{1,0:T(8,128)(2,1)S(1)}, u32[]{:S(2)}, u32[]{:S(2)}) collective-permute-start(bf16[512,512]{1,0:T(8,128)(2,1)S(1)} %add_convert_fusion.5), channel_id=1, source_target_pairs={{0,2},{1,3},{2,0},{3,1},{4,6},{5,7},{6,4},{7,5},{8,10},{9,11},{10,... | collective-permute-start | bytes 1572872 | tf_op jit(solution)/shard_map/ppermute | solution.py:38
  334.9 17.4 %collective-permute-start.73 = (bf16[512,512]{1,0:T(8,128)(2,1)}, bf16[512,512]{1,0:T(8,128)(2,1)}, u32[]{:S(2)}, u32[]{:S(2)}) collective-permute-start(bf16[512,512]{1,0:T(8,128)(2,1)} %add_convert_fusion.4), channel_id=1, source_target_pairs={{0,16},{4,20},{8,24},{12,28},{16,0},{20,4},{24,8},{28,12},{1,17},{... | collective-permute-start | bytes 1572872 | tf_op jit(solution)/shard_map/ppermute | solution.py:38
  (58 other events, 801.7 us)

commit v2 on v1

--- a/solution.py
+++ b/solution.py
@@ -84,14 +84,16 @@
     return [blocks[0]] + [swap(blocks[k], "col", k) for k in range(1, len(blocks))]
 
 
-def gather_cols(block):
+def gather_cols(block, between=None):
     size = lax.axis_size("col")
     if size != 4:
         return [(block,)] + [(swap(block, "col", k),) for k in range(1, size)]
     near = swap(block, "col", 1)
     far = swap(block, "col", 2)
-    middle = lax.ppermute(after(block, far), "col", [(1, 2), (2, 1)])
-    ends = lax.ppermute(far, "col", [(2, 3), (1, 0)])
+    later = between((near, far)) if between else ()
+    mine, passed = after((block, far), near, *later)
+    middle = lax.ppermute(mine, "col", [(1, 2), (2, 1)])
+    ends = lax.ppermute(passed, "col", [(2, 3), (1, 0)])
     return [(block,), (near,), (far,), (middle, ends)]
 
 
@@ -550,23 +552,35 @@
     tokens = gather_cols(own)
     ahead = [tokens[1][0], tokens[2][0]]
     rest = [part for entry in tokens[3:] for part in entry]
-    front_pieces = gather_rows(after(front_blocks, *last_parts(everyone)), halves=ahead, whole=rest)
-
     feed_cut = cut(cut_feed_kernel, (3, depth, units), place, down_master.T, gateup_master)
+    front_pieces = gather_rows(
+        after(front_blocks, *last_parts(everyone)), halves=ahead, whole=(*rest, *tables, feed_cut[0])
+    )
     feed_parts = exchange(list(after(tuple(feed_cut), *rest)))
 
     mixed = retain(place, decays, *tables, tokens, front_pieces)
     terms = mix(place, mixed, front_pieces, cols)
     attended = collect(terms)
     feed_blocks = join(list(after(tuple(feed_parts), terms[0])), place)
-    feed_pieces = gather_rows(feed_blocks, halves=attended[1:])
     residual = own.astype(jnp.float32) + added(attended)
-
-    def rest_of_layer(residual):
-        terms = feed(place, gather_cols(residual.astype(jnp.bfloat16)), feed_pieces)
+    feed_pieces = []
+
+    def between(first):
+        feed_pieces.extend(gather_rows(feed_blocks, halves=attended[1:], whole=first))
+        return feed_pieces[1:6:2]
+
+    mid_tokens = gather_cols(residual.astype(jnp.bfloat16), between)
+    if not feed_pieces:
+        feed_pieces = gather_rows(feed_blocks)
+
+    weights = (front_blocks[:, :width], feed_blocks[1:], front_blocks[:, width:].T, feed_blocks[0].T)
+    weights = lax.optimization_barrier(weights)
+
+    def rest_of_layer(residual, tokens, feed_pieces):
+        terms = feed(place, tokens, feed_pieces)
         return gather_rows((residual + added(collect(terms))).astype(jnp.bfloat16), direct=True)
 
-    first = rest_of_layer(residual)
+    first = rest_of_layer(residual, mid_tokens, [after(feed_pieces[0], *weights)] + feed_pieces[1:])
 
     def finish(pieces):
         return spread(place, lengths, bins, starts, pieces, rows, per_row)
@@ -576,11 +590,12 @@
             own, tables = begin(turn)
             mixed = retain(place, decays, *tables, gather_cols(own), front_pieces)
             attended = collect(mix(place, mixed, front_pieces, cols))
-            pieces = pieces + rest_of_layer(own.astype(jnp.float32) + added(attended))
+            residual = own.astype(jnp.float32) + added(attended)
+            pieces = pieces + rest_of_layer(residual, gather_cols(residual.astype(jnp.bfloat16)), feed_pieces)
         return finish(pieces)
 
     layer_output = lax.cond(count[0] > rows, more, finish, first)
-    return (layer_output, front_blocks[:, :width], feed_blocks[1:], front_blocks[:, width:].T, feed_blocks[0].T)
+    return (layer_output,) + weights
 
 
 def solution(mesh):

time: 373 us -> 365 us (0.979)
  waiting for transfers between devices: 215 us -> 210 us
    ppermute x4, waiting for transfers between devices: 33.6 us -> 17.1 us  [the longest x2 17.1 us: gather_cols(): ends = lax.ppermute(passed, 'col', [(2, 3), (1, 0)])]
    ppermute x48, waiting for transfers between devices: 162 us -> 173 us  [swap(): return lax.ppermute(block, axis, [(i, i ^ step) for i in range(size)])]
    unnamed x73 -> x59, local copies, waits for them, and re-layouts: 12.8 us -> 11 us
where the time goes in v2:
time: 365 us; the launch traced here: 361 us
  waiting for transfers between devices  210 us (58%)
  starting transfers between devices  61.4 us (17%)
  Pallas kernels  52.3 us (14%)
  local copies, waits for them, and re-layouts  23.7 us (6%)
  other arithmetic  10.2 us (3%)
    ppermute x48, waiting for transfers between devices, swap(): return lax.ppermute(block, axis, [(i, i ^ step) for i in range(size)])  173 us
    ppermute x48, starting transfers between devices, swap(): return lax.ppermute(block, axis, [(i, i ^ step) for i in range(size)])  43.6 us
    ppermute x2, waiting for transfers between devices, collect(): early = lax.ppermute(terms[3], 'col', [(3, 2), (0, 1)])  20.2 us
    ppermute x2, waiting for transfers between devices, gather_cols(): ends = lax.ppermute(passed, 'col', [(2, 3), (1, 0)])  17.1 us
    pallas_call x1, Pallas kernels, retain(): pl.pallas_call(functools.partial(retain_kernel, rows, counts, heads), out...  14.2 us
    pallas_call x1, Pallas kernels, feed(): pl.pallas_call(functools.partial(feed_kernel, rows, counts, tile), out_sh...  11.7 us
    ppermute x2, starting transfers between devices, collect(): early = lax.ppermute(terms[3], 'col', [(3, 2), (0, 1)])  11.4 us
    unnamed x59, local copies, waits for them, and re-layouts  11 us
  transfers between devices with their start and end apart: 56, of which 28 were waited for; matrix products, arithmetic and copies ran while one was open for 6% of the time, Pallas kernels for 10%

profile of v2, /device:TPU:0, one launch (start us, length us, event | category | flops | bytes accessed | tf_op | source)
XLA Modules:
  0.0 361.2 jit_solution(3355715461866248517)
XLA Ops:
  2.8 2.8 collective-permute-start.24
  16.3 3.7 %shard_map.102 = (bf16[64,4096]{1,0:T(8,128)(2,1)}, bf16[64,4096]{1,0:T(8,128)(2,1)}, bf16[64,4096]{1,0:T(8,128)(2,1)}, bf16[64,4096]{1,0:T(8,128)(2,1)}) custom-call(s32[2]{0:T(128)S(1)} %pad_add_fusion.place, f32[64,12288]{1,0:T(8,128)} %qkvg.1, f32[64,4096]{1,0:T(8,128)} %bitcast.11), custom_call_target="tpu_custom_call" | custom-call | bytes 6291456 | tf_op jit(solution)/shard_map/pallas_call | solution.py:138
  21.5 2.6 collective-permute-start.32
  24.4 16.2 %collective-permute-done.31.refs_1_ = bf16[64,4096]{1,0:T(8,128)(2,1)S(1)} collective-permute-done((bf16[64,4096]{1,0:T(8,128)(2,1)}, bf16[64,4096]{1,0:T(8,128)(2,1)S(1)}, u32[]{:S(2)}, u32[]{:S(2)}) %collective-permute-start.31) | collective-permute-done | bytes 524320 | tf_op jit(solution)/shard_map/ppermute | solution.py:38
  40.6 19.4 %collective-permute-done.32.refs_2_ = bf16[64,4096]{1,0:T(8,128)(2,1)S(1)} collective-permute-done((bf16[64,4096]{1,0:T(8,128)(2,1)}, bf16[64,4096]{1,0:T(8,128)(2,1)S(1)}, u32[]{:S(2)}, u32[]{:S(2)}) %collective-permute-start.32) | collective-permute-done | bytes 524320 | tf_op jit(solution)/shard_map/ppermute | solution.py:38
  64.9 6.5 %collective-permute-done.34 = bf16[512,512]{1,0:T(8,128)(2,1)S(1)} collective-permute-done((bf16[512,512]{1,0:T(8,128)(2,1)S(1)}, bf16[512,512]{1,0:T(8,128)(2,1)S(1)}, u32[]{:S(2)}, u32[]{:S(2)}) %collective-permute-start.34) | collective-permute-done | bytes 524320 | tf_op jit(solution)/shard_map/ppermute | solution.py:38
  75.8 4.1 %shard_map.101 = (s32[64]{0:T(128)S(1)}, s32[16]{0:T(128)S(1)}, s32[16]{0:T(128)S(1)}, s32[1]{0:T(128)}) custom-call(s32[2]{0:T(128)S(1)} %pad_add_fusion.place, s32[16]{0:T(128)} %pad_add_fusion.3.lengths), custom_call_target="tpu_custom_call" | custom-call | tf_op jit(solution)/shard_map/pallas_call | solution.py:223
  81.3 3.2 shard_map.103.refs_0_
  84.6 3.0 collective-permute-start.36
  87.7 23.2 %collective-permute-done.37.refs_2_ = bf16[512,512]{1,0:T(8,128)(2,1)} collective-permute-done((bf16[512,512]{1,0:T(8,128)(2,1)}, bf16[512,512]{1,0:T(8,128)(2,1)}, u32[]{:S(2)}, u32[]{:S(2)}) %collective-permute-start.37) | collective-permute-done | bytes 524320 | tf_op jit(solution)/shard_map/ppermute | solution.py:38
  111.0 4.5 %collective-permute-done.42.refs_9_.refs_4_ = bf16[256,4096]{1,0:T(8,128)(2,1)S(1)} collective-permute-done((bf16[256,4096]{1,0:T(8,128)(2,1)S(1)}, bf16[256,4096]{1,0:T(8,128)(2,1)S(1)}, u32[]{:S(2)}, u32[]{:S(2)}) %collective-permute-start.42) | collective-permute-done | bytes 2097184 | tf_op jit(solution)/shard_map/ppermute | solution.py:38
  120.5 3.2 shard_map.105
  130.0 6.6 %collective-permute-done.39.refs_4_ = bf16[512,512]{1,0:T(8,128)(2,1)} collective-permute-done((bf16[512,512]{1,0:T(8,128)(2,1)}, bf16[512,512]{1,0:T(8,128)(2,1)}, u32[]{:S(2)}, u32[]{:S(2)}) %collective-permute-start.39) | collective-permute-done | bytes 524320 | tf_op jit(solution)/shard_map/ppermute | solution.py:96
  149.3 14.2 %shard_map.106.mixed = bf16[512,1024]{1,0:T(8,128)(2,1)} custom-call(s32[2]{0:T(128)S(1)} %pad_add_fusion.place, f32[2]{0:T(128)S(1)} %negate_log-plus-one_fusion.decays, f32[512,128]{1,0:T(8,128)} %get-tuple-element.311.cosine, f32[512,128]{1,0:T(8,128)} %get-tuple-element.310.sine, s32[512,1]{1,0:T(8,128)} %copy.14.seg_col, ...), custom_call_target="tpu_custom_call" | custom-call | flops 8375186432 | bytes 12582912 | tf_op jit(solution)/shard_map/pallas_call | solution.py:402
  163.6 6.2 %shard_map.107 = (bf16[512,512]{1,0:T(8,128)(2,1)}, bf16[512,512]{1,0:T(8,128)(2,1)}, bf16[512,512]{1,0:T(8,128)(2,1)}, bf16[512,512]{1,0:T(8,128)(2,1)}) custom-call(s32[2]{0:T(128)S(1)} %pad_add_fusion.place, bf16[512,1024]{1,0:T(8,128)(2,1)} %shard_map.106.mixed, bf16[256,4096]{1,0:T(8,128)(2,1)S(1)} %shard_map.104.refs_5_.refs_0_, ...), custom_call_target="tpu_custom_call" | custom-call | flops 2147483648 | bytes 4194304 | tf_op jit(solution)/shard_map/pallas_call | solution.py:447
  169.8 5.1 %collective-permute-done.56.refs_2_ = bf16[3,64,1024]{2,1,0:T(8,128)(2,1)S(1)} collective-permute-done((bf16[3,64,1024]{2,1,0:T(8,128)(2,1)}, bf16[3,64,1024]{2,1,0:T(8,128)(2,1)S(1)}, u32[]{:S(2)}, u32[]{:S(2)}) %collective-permute-start.56) | collective-permute-done | bytes 393248 | tf_op jit(solution)/shard_map/ppermute | solution.py:38
  180.6 9.9 %collective-permute-start.49 = (bf16[512,512]{1,0:T(8,128)(2,1)}, bf16[512,512]{1,0:T(8,128)(2,1)S(1)}, u32[]{:S(2)}, u32[]{:S(2)}) collective-permute-start(bf16[512,512]{1,0:T(8,128)(2,1)} %get-tuple-element.264), channel_id=1, source_target_pairs={{3,2},{0,1},{7,6},{4,5},{11,10},{8,9},{15,14},{12,13},{19,18},{16,... | collective-permute-start | bytes 1572872 | tf_op jit(solution)/shard_map/ppermute | solution.py:103
  191.4 9.9 %collective-permute-done.49 = bf16[512,512]{1,0:T(8,128)(2,1)S(1)} collective-permute-done((bf16[512,512]{1,0:T(8,128)(2,1)}, bf16[512,512]{1,0:T(8,128)(2,1)S(1)}, u32[]{:S(2)}, u32[]{:S(2)}) %collective-permute-start.49) | collective-permute-done | bytes 524320 | tf_op jit(solution)/shard_map/ppermute | solution.py:103
  203.9 19.7 %collective-permute-done.50 = bf16[512,512]{1,0:T(8,128)(2,1)S(1)} collective-permute-done((bf16[512,512]{1,0:T(8,128)(2,1)S(1)}, bf16[512,512]{1,0:T(8,128)(2,1)S(1)}, u32[]{:S(2)}, u32[]{:S(2)}) %collective-permute-start.50) | collective-permute-done | bytes 524320 | tf_op jit(solution)/shard_map/ppermute | solution.py:38
  223.6 4.2 %collective-permute-done.51 = bf16[512,512]{1,0:T(8,128)(2,1)S(1)} collective-permute-done((bf16[512,512]{1,0:T(8,128)(2,1)S(1)}, bf16[512,512]{1,0:T(8,128)(2,1)S(1)}, u32[]{:S(2)}, u32[]{:S(2)}) %collective-permute-start.51) | collective-permute-done | bytes 524320 | tf_op jit(solution)/shard_map/ppermute | solution.py:38
  232.6 18.3 %collective-permute-done.54.refs_2_ = bf16[512,512]{1,0:T(8,128)(2,1)S(1)} collective-permute-done((bf16[512,512]{1,0:T(8,128)(2,1)S(1)}, bf16[512,512]{1,0:T(8,128)(2,1)S(1)}, u32[]{:S(2)}, u32[]{:S(2)}) %collective-permute-start.54) | collective-permute-done | bytes 524320 | tf_op jit(solution)/shard_map/ppermute | solution.py:38
  254.3 4.5 %collective-permute-done.61.refs_8_ = bf16[3,256,1024]{2,1,0:T(8,128)(2,1)S(1)} collective-permute-done((bf16[3,256,1024]{2,1,0:T(8,128)(2,1)S(1)}, bf16[3,256,1024]{2,1,0:T(8,128)(2,1)S(1)}, u32[]{:S(2)}, u32[]{:S(2)}) %collective-permute-start.61) | collective-permute-done | bytes 1572896 | tf_op jit(solution)/shard_map/ppermute | solution.py:38
  264.8 10.5 %collective-permute-done.64.refs_4_ = bf16[512,512]{1,0:T(8,128)(2,1)S(1)} collective-permute-done((bf16[512,512]{1,0:T(8,128)(2,1)S(1)}, bf16[512,512]{1,0:T(8,128)(2,1)S(1)}, u32[]{:S(2)}, u32[]{:S(2)}) %collective-permute-start.64) | collective-permute-done | bytes 524320 | tf_op jit(solution)/shard_map/ppermute | solution.py:96
  276.2 11.7 %shard_map.109 = (bf16[512,512]{1,0:T(8,128)(2,1)}, bf16[512,512]{1,0:T(8,128)(2,1)}, bf16[512,512]{1,0:T(8,128)(2,1)}, bf16[512,512]{1,0:T(8,128)(2,1)}) custom-call(s32[2]{0:T(128)S(1)} %pad_add_fusion.place, bf16[512,512]{1,0:T(8,128)(2,1)} %copy-done.24, bf16[512,512]{1,0:T(8,128)(2,1)} %copy-done.39, bf16[512,512]{1,0:T(8,128)(2,1)} %copy-done.38, ...), custom_call_target="tpu_custom_call" | custom-call | flops 6442450944 | bytes 12582912 | tf_op jit(solution)/shard_map/pallas_call | solution.py:503
  290.1 10.3 %collective-permute-done.68 = bf16[512,512]{1,0:T(8,128)(2,1)S(1)} collective-permute-done((bf16[512,512]{1,0:T(8,128)(2,1)}, bf16[512,512]{1,0:T(8,128)(2,1)S(1)}, u32[]{:S(2)}, u32[]{:S(2)}) %collective-permute-start.68) | collective-permute-done | bytes 524320 | tf_op jit(solution)/shard_map/ppermute | solution.py:103
  304.1 18.5 %collective-permute-done.69 = bf16[512,512]{1,0:T(8,128)(2,1)S(1)} collective-permute-done((bf16[512,512]{1,0:T(8,128)(2,1)}, bf16[512,512]{1,0:T(8,128)(2,1)S(1)}, u32[]{:S(2)}, u32[]{:S(2)}) %collective-permute-start.69) | collective-permute-done | bytes 524320 | tf_op jit(solution)/shard_map/ppermute | solution.py:38
  322.5 5.7 %collective-permute-done.70 = bf16[512,512]{1,0:T(8,128)(2,1)S(1)} collective-permute-done((bf16[512,512]{1,0:T(8,128)(2,1)S(1)}, bf16[512,512]{1,0:T(8,128)(2,1)S(1)}, u32[]{:S(2)}, u32[]{:S(2)}) %collective-permute-start.70) | collective-permute-done | bytes 524320 | tf_op jit(solution)/shard_map/ppermute | solution.py:38
  328.3 2.6 add_convert_fusion.4
  334.4 10.8 %collective-permute-done.77 = bf16[512,512]{1,0:T(8,128)(2,1)} collective-permute-done((bf16[512,512]{1,0:T(8,128)(2,1)}, bf16[512,512]{1,0:T(8,128)(2,1)}, u32[]{:S(2)}, u32[]{:S(2)}) %collective-permute-start.77) | collective-permute-done | bytes 524320 | tf_op jit(solution)/shard_map/ppermute | solution.py:38
  345.2 5.5 %collective-permute-done.73 = bf16[512,512]{1,0:T(8,128)(2,1)} collective-permute-done((bf16[512,512]{1,0:T(8,128)(2,1)}, bf16[512,512]{1,0:T(8,128)(2,1)}, u32[]{:S(2)}, u32[]{:S(2)}) %collective-permute-start.73) | collective-permute-done | bytes 524320 | tf_op jit(solution)/shard_map/ppermute | solution.py:38
  355.9 3.8 %conditional.1 = (bf16[1024,512]{1,0:T(8,128)(2,1)S(1)}) conditional(s32[]{:T(128)} %bitcast.2, (s32[2]{0:T(128)S(1)}, s32[2]{0:T(128)S(1)}, s32[16]{0:T(128)S(1)}, s32[16]{0:T(128)S(1)}, bf16[512,512]{1,0:T(8,128)(2,1)}, /*index=5*/bf16[512,512]{1,0:T(8,128)(2,1)}, bf16[512,512]{1,0:T(8,128)(2,1)}, bf16[512,512]{1,0:T(8,128)(2,1)}, ...), branch_computations={%region_0.1_spmd, %region_1.2_spmd} | conditional | flops 16974625792 | bytes 171464288 | solution.py:597
  355.9 2.7 branch_0_fun.1
  (182 shorter events, 88.3 us)
Async XLA Ops:
  12.7 47.3 %collective-permute-start.27 = (bf16[1024,512]{1,0:T(8,128)(2,1)}, bf16[1024,512]{1,0:T(8,128)(2,1)S(1)}, u32[]{:S(2)}, u32[]{:S(2)}) collective-permute-start(bf16[1024,512]{1,0:T(8,128)(2,1)} %refs_0_), channel_id=1, source_target_pairs={{0,16},{4,20},{8,24},{12,28},{16,0},{20,4},{24,8},{28,12},{1,17},{... | collective-permute-start | bytes 3145736 | tf_op jit(solution)/shard_map/ppermute | solution.py:38
  14.7 45.3 %collective-permute-start.26 = (bf16[1024,512]{1,0:T(8,128)(2,1)}, bf16[1024,512]{1,0:T(8,128)(2,1)}, u32[]{:S(2)}, u32[]{:S(2)}) collective-permute-start(bf16[1024,512]{1,0:T(8,128)(2,1)} %refs_0_), channel_id=1, source_target_pairs={{0,8},{4,12},{8,0},{12,4},{16,24},{20,28},{24,16},{28,20},{1,9},{5... | collective-permute-start | bytes 3145736 | tf_op jit(solution)/shard_map/ppermute | solution.py:38
  20.0 20.6 %collective-permute-start.31 = (bf16[64,4096]{1,0:T(8,128)(2,1)}, bf16[64,4096]{1,0:T(8,128)(2,1)S(1)}, u32[]{:S(2)}, u32[]{:S(2)}) collective-permute-start(bf16[64,4096]{1,0:T(8,128)(2,1)} %get-tuple-element.245), channel_id=1, source_target_pairs={{0,1},{1,0},{2,3},{3,2},{4,5},{5,4},{6,7},{7,6},{8,9},{9,8},{10,11... | collective-permute-start | bytes 1572872 | tf_op jit(solution)/shard_map/ppermute | solution.py:38
  21.5 38.4 %collective-permute-start.32 = (bf16[64,4096]{1,0:T(8,128)(2,1)}, bf16[64,4096]{1,0:T(8,128)(2,1)S(1)}, u32[]{:S(2)}, u32[]{:S(2)}) collective-permute-start(bf16[64,4096]{1,0:T(8,128)(2,1)} %get-tuple-element.246), channel_id=1, source_target_pairs={{0,2},{1,3},{2,0},{3,1},{4,6},{5,7},{6,4},{7,5},{8,10},{9,11},{10,... | collective-permute-start | bytes 1572872 | tf_op jit(solution)/shard_map/ppermute | solution.py:38
  24.1 38.2 %collective-permute-start.40 = (bf16[64,4096]{1,0:T(8,128)(2,1)}, bf16[64,4096]{1,0:T(8,128)(2,1)S(1)}, u32[]{:S(2)}, u32[]{:S(2)}) collective-permute-start(bf16[64,4096]{1,0:T(8,128)(2,1)} %get-tuple-element.254), channel_id=1, source_target_pairs={{0,3},{1,2},{2,1},{3,0},{4,7},{5,6},{6,5},{7,4},{8,11},{9,10},{10,... | collective-permute-start | bytes 1572872 | tf_op jit(solution)/shard_map/ppermute | solution.py:38
  73.0 42.5 %collective-permute-start.42 = (bf16[256,4096]{1,0:T(8,128)(2,1)S(1)}, bf16[256,4096]{1,0:T(8,128)(2,1)S(1)}, u32[]{:S(2)}, u32[]{:S(2)}) collective-permute-start(bf16[256,4096]{1,0:T(8,128)(2,1)S(1)} %shard_map.104.refs_5_.refs_0_), channel_id=1, source_target_pairs={{0,16},{4,20},{8,24},{12,28},{16,0},{20,4},{24,8},{28,12},{1,17},{... | collective-permute-start | bytes 6291464 | tf_op jit(solution)/shard_map/ppermute | solution.py:38
  75.3 40.7 %collective-permute-start.41 = (bf16[256,4096]{1,0:T(8,128)(2,1)S(1)}, bf16[256,4096]{1,0:T(8,128)(2,1)S(1)}, u32[]{:S(2)}, u32[]{:S(2)}) collective-permute-start(bf16[256,4096]{1,0:T(8,128)(2,1)S(1)} %shard_map.104.refs_5_.refs_0_), channel_id=1, source_target_pairs={{0,8},{4,12},{8,0},{12,4},{16,24},{20,28},{24,16},{28,20},{1,9},{5... | collective-permute-start | bytes 6291464 | tf_op jit(solution)/shard_map/ppermute | solution.py:38
  84.5 26.3 %collective-permute-start.37 = (bf16[512,512]{1,0:T(8,128)(2,1)}, bf16[512,512]{1,0:T(8,128)(2,1)}, u32[]{:S(2)}, u32[]{:S(2)}) collective-permute-start(bf16[512,512]{1,0:T(8,128)(2,1)} %shard_map.103.refs_0_), channel_id=1, source_target_pairs={{0,2},{1,3},{2,0},{3,1},{4,6},{5,7},{6,4},{7,5},{8,10},{9,11},{10,... | collective-permute-start | bytes 1572872 | tf_op jit(solution)/shard_map/ppermute | solution.py:38
  84.6 26.3 %collective-permute-start.36 = (bf16[512,512]{1,0:T(8,128)(2,1)}, bf16[512,512]{1,0:T(8,128)(2,1)S(1)}, u32[]{:S(2)}, u32[]{:S(2)}) collective-permute-start(bf16[512,512]{1,0:T(8,128)(2,1)} %shard_map.103.refs_0_), channel_id=1, source_target_pairs={{0,1},{1,0},{2,3},{3,2},{4,5},{5,4},{6,7},{7,6},{8,9},{9,8},{10,11... | collective-permute-start | bytes 1572872 | tf_op jit(solution)/shard_map/ppermute | solution.py:38
  118.4 20.7 %collective-permute-start.47 = (bf16[128,4096]{1,0:T(8,128)(2,1)}, bf16[128,4096]{1,0:T(8,128)(2,1)}, u32[]{:S(2)}, u32[]{:S(2)}) collective-permute-start(bf16[128,4096]{1,0:T(8,128)(2,1)} %slice.40), channel_id=1, source_target_pairs={{0,16},{4,20},{8,24},{12,28},{16,0},{20,4},{24,8},{28,12},{1,17},{... | collective-permute-start | bytes 3145736 | tf_op jit(solution)/shard_map/ppermute | solution.py:38
  119.7 19.7 %collective-permute-start.46 = (bf16[128,4096]{1,0:T(8,128)(2,1)}, bf16[128,4096]{1,0:T(8,128)(2,1)}, u32[]{:S(2)}, u32[]{:S(2)}) collective-permute-start(bf16[128,4096]{1,0:T(8,128)(2,1)} %slice.39), channel_id=1, source_target_pairs={{0,8},{4,12},{8,0},{12,4},{16,24},{20,28},{24,16},{28,20},{1,9},{5... | collective-permute-start | bytes 3145736 | tf_op jit(solution)/shard_map/ppermute | solution.py:38
  129.5 15.4 %collective-permute-start.45 = (bf16[256,4096]{1,0:T(8,128)(2,1)}, bf16[256,4096]{1,0:T(8,128)(2,1)}, u32[]{:S(2)}, u32[]{:S(2)}) collective-permute-start(bf16[256,4096]{1,0:T(8,128)(2,1)} %copy-done), channel_id=1, source_target_pairs={{0,4},{4,0},{8,12},{12,8},{16,20},{20,16},{24,28},{28,24},{1,5},{5... | collective-permute-start | bytes 6291464 | tf_op jit(solution)/shard_map/ppermute | solution.py:38
  129.5 17.6 %collective-permute-start.43 = (bf16[256,4096]{1,0:T(8,128)(2,1)S(1)}, bf16[256,4096]{1,0:T(8,128)(2,1)}, u32[]{:S(2)}, u32[]{:S(2)}) collective-permute-start(bf16[256,4096]{1,0:T(8,128)(2,1)S(1)} %shard_map.104.refs_5_.refs_0_), channel_id=1, source_target_pairs={{0,4},{4,0},{8,12},{12,8},{16,20},{20,16},{24,28},{28,24},{1,5},{5... | collective-permute-start | bytes 6291464 | tf_op jit(solution)/shard_map/ppermute | solution.py:38
  144.9 24.9 %collective-permute-start.55 = (bf16[3,64,1024]{2,1,0:T(8,128)(2,1)}, bf16[3,64,1024]{2,1,0:T(8,128)(2,1)S(1)}, u32[]{:S(2)}, u32[]{:S(2)}) collective-permute-start(bf16[3,64,1024]{2,1,0:T(8,128)(2,1)} %get-tuple-element.271), channel_id=1, source_target_pairs={{0,1},{1,0},{2,3},{3,2},{4,5},{5,4},{6,7},{7,6},{8,9},{9,8},{10,11... | collective-permute-start | bytes 1179656 | tf_op jit(solution)/shard_map/ppermute | solution.py:38
  144.9 30.0 %collective-permute-start.56 = (bf16[3,64,1024]{2,1,0:T(8,128)(2,1)}, bf16[3,64,1024]{2,1,0:T(8,128)(2,1)S(1)}, u32[]{:S(2)}, u32[]{:S(2)}) collective-permute-start(bf16[3,64,1024]{2,1,0:T(8,128)(2,1)} %get-tuple-element.272), channel_id=1, source_target_pairs={{0,2},{1,3},{2,0},{3,1},{4,6},{5,7},{6,4},{7,5},{8,10},{9,11},{10,... | collective-permute-start | bytes 1179656 | tf_op jit(solution)/shard_map/ppermute | solution.py:38
  147.1 27.8 %collective-permute-start.57 = (bf16[3,64,1024]{2,1,0:T(8,128)(2,1)}, bf16[3,64,1024]{2,1,0:T(8,128)(2,1)}, u32[]{:S(2)}, u32[]{:S(2)}) collective-permute-start(bf16[3,64,1024]{2,1,0:T(8,128)(2,1)} %get-tuple-element.273), channel_id=1, source_target_pairs={{0,3},{1,2},{2,1},{3,0},{4,7},{5,6},{6,5},{7,4},{8,11},{9,10},{10,... | collective-permute-start | bytes 1179656 | tf_op jit(solution)/shard_map/ppermute | solution.py:38
  177.1 50.7 %collective-permute-start.59 = (bf16[3,256,1024]{2,1,0:T(8,128)(2,1)S(1)}, bf16[3,256,1024]{2,1,0:T(8,128)(2,1)S(1)}, u32[]{:S(2)}, u32[]{:S(2)}) collective-permute-start(bf16[3,256,1024]{2,1,0:T(8,128)(2,1)S(1)} %shard_map.108.refs_5_), channel_id=1, source_target_pairs={{0,16},{4,20},{8,24},{12,28},{16,0},{20,4},{24,8},{28,12},{1,17},{... | collective-permute-start | bytes 4718600 | tf_op jit(solution)/shard_map/ppermute | solution.py:38
  178.9 49.0 %collective-permute-start.58 = (bf16[3,256,1024]{2,1,0:T(8,128)(2,1)S(1)}, bf16[3,256,1024]{2,1,0:T(8,128)(2,1)S(1)}, u32[]{:S(2)}, u32[]{:S(2)}) collective-permute-start(bf16[3,256,1024]{2,1,0:T(8,128)(2,1)S(1)} %shard_map.108.refs_5_), channel_id=1, source_target_pairs={{0,8},{4,12},{8,0},{12,4},{16,24},{20,28},{24,16},{28,20},{1,9},{5... | collective-permute-start | bytes 4718600 | tf_op jit(solution)/shard_map/ppermute | solution.py:38
  180.6 20.7 %collective-permute-start.49 = (bf16[512,512]{1,0:T(8,128)(2,1)}, bf16[512,512]{1,0:T(8,128)(2,1)S(1)}, u32[]{:S(2)}, u32[]{:S(2)}) collective-permute-start(bf16[512,512]{1,0:T(8,128)(2,1)} %get-tuple-element.264), channel_id=1, source_target_pairs={{3,2},{0,1},{7,6},{4,5},{11,10},{8,9},{15,14},{12,13},{19,18},{16,... | collective-permute-start | bytes 1572872 | tf_op jit(solution)/shard_map/ppermute | solution.py:103
  201.3 22.3 %collective-permute-start.50 = (bf16[512,512]{1,0:T(8,128)(2,1)S(1)}, bf16[512,512]{1,0:T(8,128)(2,1)S(1)}, u32[]{:S(2)}, u32[]{:S(2)}) collective-permute-start(bf16[512,512]{1,0:T(8,128)(2,1)S(1)} %copy-done.40), channel_id=1, source_target_pairs={{0,1},{1,0},{2,3},{3,2},{4,5},{5,4},{6,7},{7,6},{8,9},{9,8},{10,11... | collective-permute-start | bytes 1572872 | tf_op jit(solution)/shard_map/ppermute | solution.py:38
  203.8 24.0 %collective-permute-start.51 = (bf16[512,512]{1,0:T(8,128)(2,1)S(1)}, bf16[512,512]{1,0:T(8,128)(2,1)S(1)}, u32[]{:S(2)}, u32[]{:S(2)}) collective-permute-start(bf16[512,512]{1,0:T(8,128)(2,1)S(1)} %add_convert_fusion.6), channel_id=1, source_target_pairs={{0,2},{1,3},{2,0},{3,1},{4,6},{5,7},{6,4},{7,5},{8,10},{9,11},{10,... | collective-permute-start | bytes 1572872 | tf_op jit(solution)/shard_map/ppermute | solution.py:38
  228.0 23.5 %collective-permute-start.66 = (bf16[3,128,1024]{2,1,0:T(8,128)(2,1)S(1)}, bf16[3,128,1024]{2,1,0:T(8,128)(2,1)S(1)}, u32[]{:S(2)}, u32[]{:S(2)}) collective-permute-start(bf16[3,128,1024]{2,1,0:T(8,128)(2,1)S(1)} %slice.46), channel_id=1, source_target_pairs={{0,16},{4,20},{8,24},{12,28},{16,0},{20,4},{24,8},{28,12},{1,17},{... | collective-permute-start | bytes 2359304 | tf_op jit(solution)/shard_map/ppermute | solution.py:38
  228.4 23.5 %collective-permute-start.65 = (bf16[3,128,1024]{2,1,0:T(8,128)(2,1)S(1)}, bf16[3,128,1024]{2,1,0:T(8,128)(2,1)S(1)}, u32[]{:S(2)}, u32[]{:S(2)}) collective-permute-start(bf16[3,128,1024]{2,1,0:T(8,128)(2,1)S(1)} %slice.45), channel_id=1, source_target_pairs={{0,8},{4,12},{8,0},{12,4},{16,24},{20,28},{24,16},{28,20},{1,9},{5... | collective-permute-start | bytes 2359304 | tf_op jit(solution)/shard_map/ppermute | solution.py:38
  230.3 20.6 %collective-permute-start.54 = (bf16[512,512]{1,0:T(8,128)(2,1)S(1)}, bf16[512,512]{1,0:T(8,128)(2,1)S(1)}, u32[]{:S(2)}, u32[]{:S(2)}) collective-permute-start(bf16[512,512]{1,0:T(8,128)(2,1)S(1)} %fusion.3.refs_0_), channel_id=1, source_target_pairs={{0,2},{1,3},{2,0},{3,1},{4,6},{5,7},{6,4},{7,5},{8,10},{9,11},{10,... | collective-permute-start | bytes 1572872 | tf_op jit(solution)/shard_map/ppermute | solution.py:38
  230.5 20.5 %collective-permute-start.53 = (bf16[512,512]{1,0:T(8,128)(2,1)S(1)}, bf16[512,512]{1,0:T(8,128)(2,1)S(1)}, u32[]{:S(2)}, u32[]{:S(2)}) collective-permute-start(bf16[512,512]{1,0:T(8,128)(2,1)S(1)} %fusion.3.refs_0_), channel_id=1, source_target_pairs={{0,1},{1,0},{2,3},{3,2},{4,5},{5,4},{6,7},{7,6},{8,9},{9,8},{10,11... | collective-permute-start | bytes 1572872 | tf_op jit(solution)/shard_map/ppermute | solution.py:38
  232.6 19.8 %collective-permute-start.62 = (bf16[3,256,1024]{2,1,0:T(8,128)(2,1)S(1)}, bf16[3,256,1024]{2,1,0:T(8,128)(2,1)S(1)}, u32[]{:S(2)}, u32[]{:S(2)}) collective-permute-start(bf16[3,256,1024]{2,1,0:T(8,128)(2,1)S(1)} %collective-permute-done.59.refs_9_), channel_id=1, source_target_pairs={{0,4},{4,0},{8,12},{12,8},{16,20},{20,16},{24,28},{28,24},{1,5},{5... | collective-permute-start | bytes 4718600 | tf_op jit(solution)/shard_map/ppermute | solution.py:38
  252.0 24.2 %collective-permute-start.67 = (bf16[3,256,1024]{2,1,0:T(8,128)(2,1)S(1)}, bf16[3,256,1024]{2,1,0:T(8,128)(2,1)}, u32[]{:S(2)}, u32[]{:S(2)}) collective-permute-start(bf16[3,256,1024]{2,1,0:T(8,128)(2,1)S(1)} %constant_dynamic-update-slice_fusion.4.refs_11_), channel_id=1, source_target_pairs={{0,4},{4,0},{8,12},{12,8},{16,20},{20,16},{24,28},{28,24},{1,5},{5... | collective-permute-start | bytes 4718600 | tf_op jit(solution)/shard_map/ppermute | solution.py:38
  259.5 15.9 %collective-permute-start.64 = (bf16[512,512]{1,0:T(8,128)(2,1)S(1)}, bf16[512,512]{1,0:T(8,128)(2,1)S(1)}, u32[]{:S(2)}, u32[]{:S(2)}) collective-permute-start(bf16[512,512]{1,0:T(8,128)(2,1)S(1)} %collective-permute-done.54.refs_2_), channel_id=1, source_target_pairs={{2,3},{1,0},{6,7},{5,4},{10,11},{9,8},{14,15},{13,12},{18,19},{17,... | collective-permute-start | bytes 1572872 | tf_op jit(solution)/shard_map/ppermute | solution.py:96
  300.4 22.1 %collective-permute-start.69 = (bf16[512,512]{1,0:T(8,128)(2,1)}, bf16[512,512]{1,0:T(8,128)(2,1)S(1)}, u32[]{:S(2)}, u32[]{:S(2)}) collective-permute-start(bf16[512,512]{1,0:T(8,128)(2,1)} %get-tuple-element.293), channel_id=1, source_target_pairs={{0,1},{1,0},{2,3},{3,2},{4,5},{5,4},{6,7},{7,6},{8,9},{9,8},{10,11... | collective-permute-start | bytes 1572872 | tf_op jit(solution)/shard_map/ppermute | solution.py:38
  304.0 24.3 %collective-permute-start.70 = (bf16[512,512]{1,0:T(8,128)(2,1)S(1)}, bf16[512,512]{1,0:T(8,128)(2,1)S(1)}, u32[]{:S(2)}, u32[]{:S(2)}) collective-permute-start(bf16[512,512]{1,0:T(8,128)(2,1)S(1)} %add_convert_fusion.5), channel_id=1, source_target_pairs={{0,2},{1,3},{2,0},{3,1},{4,6},{5,7},{6,4},{7,5},{8,10},{9,11},{10,... | collective-permute-start | bytes 1572872 | tf_op jit(solution)/shard_map/ppermute | solution.py:38
  333.3 17.3 %collective-permute-start.73 = (bf16[512,512]{1,0:T(8,128)(2,1)}, bf16[512,512]{1,0:T(8,128)(2,1)}, u32[]{:S(2)}, u32[]{:S(2)}) collective-permute-start(bf16[512,512]{1,0:T(8,128)(2,1)} %add_convert_fusion.4), channel_id=1, source_target_pairs={{0,16},{4,20},{8,24},{12,28},{16,0},{20,4},{24,8},{28,12},{1,17},{... | collective-permute-start | bytes 1572872 | tf_op jit(solution)/shard_map/ppermute | solution.py:38
  333.7 17.0 %collective-permute-start.72 = (bf16[512,512]{1,0:T(8,128)(2,1)}, bf16[512,512]{1,0:T(8,128)(2,1)}, u32[]{:S(2)}, u32[]{:S(2)}) collective-permute-start(bf16[512,512]{1,0:T(8,128)(2,1)} %add_convert_fusion.4), channel_id=1, source_target_pairs={{0,8},{4,12},{8,0},{12,4},{16,24},{20,28},{24,16},{28,20},{1,9},{5... | collective-permute-start | bytes 1572872 | tf_op jit(solution)/shard_map/ppermute | solution.py:38
  (51 other events, 604.9 us)
